TPU v7x, 128 devices: a whole 4x4x4 slice. The times are simulated.
128 devices in a mesh: win: 4 (over y), seq: 16 (over z, x), heads: 2 (over core).
Axes of the slice: x: 4, y: 4, z: 4, core: 2. Of those that a mesh axis runs over, the one named last changes fastest.
Arguments:
- tokens: bfloat16 [4, 8192, 768], P('win', ('seq', 'heads')), may hold values from -6 to 6
- first_gain: float32 [768], replicated, may hold values from 0.5 to 1.5
- first_shift: float32 [768], replicated, may hold values from -1.75 to 1.75
- query_weight: bfloat16 [768, 768], P(None, 'heads'), may hold values from -0.5 to 0.5
- query_bias: float32 [768], P('heads'), may hold values from -3 to 3
- keyval_weight: bfloat16 [768, 128], replicated, may hold values from -0.21875 to 0.21875
- value_bias: float32 [64], replicated, may hold values from -1.75 to 1.75
- out_weight: bfloat16 [768, 768], P('heads'), may hold values from -0.4375 to 0.4375
- out_bias: float32 [768], replicated, may hold values from -1.75 to 1.75
- second_gain: float32 [768], replicated, may hold values from 0.5 to 1.5
- second_shift: float32 [768], replicated, may hold values from -1.75 to 1.75
- expand_weight: bfloat16 [768, 3072], P(None, 'heads'), may hold values from -0.21875 to 0.21875
- expand_bias: float32 [3072], P('heads'), may hold values from -1.75 to 1.75
- contract_weight: bfloat16 [3072, 768], P('heads'), may hold values from -0.109375 to 0.109375
- contract_bias: float32 [768], replicated, may hold values from -1.75 to 1.75
- cotangent: bfloat16 [4, 8192, 768], P('win', ('seq', 'heads')), may hold values from -6 to 6
- lengths: int32 [4, 8], P('win'), may hold values from 1 to 8064, 8192 in all within a row
Outputs:
- block_out: bfloat16 [4, 8192, 768], P('win', ('seq', 'heads'))
- tokens_grad: float32 [4, 8192, 768], P('win', ('seq', 'heads'))
- first_gain_grad: float32 [768], replicated
- first_shift_grad: float32 [768], replicated
- query_weight_grad: float32 [768, 768], P(None, 'heads')
- query_bias_grad: float32 [768], P('heads')
- keyval_weight_grad: float32 [768, 128], replicated
- value_bias_grad: float32 [64], replicated
- out_weight_grad: float32 [768, 768], P('heads')
- out_bias_grad: float32 [768], replicated
- second_gain_grad: float32 [768], replicated
- second_shift_grad: float32 [768], replicated
- expand_weight_grad: float32 [768, 3072], P(None, 'heads')
- expand_bias_grad: float32 [3072], P('heads')
- contract_weight_grad: float32 [3072, 768], P('heads')
- contract_bias_grad: float32 [768], replicated
Inputs may be any that keep to these rules, and one draw needn't show every extreme that they name: In each window the 8 file lengths add up to 8192, and the longest file has exactly 8064 tokens.
All inputs are finite; a program needn't handle non-finite values.
Results may differ from a plain program's by a relative error of at most 0.018.
Values may be sent and summed in bfloat16 or wider, within the bound.
No kernel may reach another device: no remote copies, remote signals or barrier semaphores. Data moves between devices by JAX's collectives and lax.ppermute only.
A program may use at most 192 MiB of HBM per device.

v0:
```python
import math
import jax
import jax.numpy as jnp
from jax import lax
from jax.experimental import pallas as pl
from jax.experimental.pallas import tpu as pltpu
from jax.sharding import PartitionSpec as P

DH = 64
NEG = -1e30
TILE = 256
LANES = 256
HALF = 128


def mm(left, right):
    return lax.dot_general(left, right, (((1,), (0,)), ((), ())), preferred_element_type=jnp.float32)


def pieces(row, width):
    high = row.astype(jnp.bfloat16).astype(jnp.float32)
    rest = row - high
    mid = rest.astype(jnp.bfloat16).astype(jnp.float32)
    low = rest - mid
    which = lax.broadcasted_iota(jnp.int32, (16, width), 0)
    block = jnp.where(which == 0, -high, jnp.where(which == 1, -mid, jnp.where(which == 2, -low, 0.0)))
    return block.astype(jnp.bfloat16)


def with_ones(part):
    lane = lax.broadcasted_iota(jnp.int32, (part.shape[0], HALF), 1)
    wide = jnp.concatenate([part, jnp.zeros_like(part)], axis=1)
    return jnp.where((lane >= DH) & (lane < DH + 3), jnp.ones_like(wide), wide)


def mask_of(tile, chunk_pos, starts):
    key = tile * TILE + lax.broadcasted_iota(jnp.int32, (TILE, HALF), 0)
    query = chunk_pos + lax.broadcasted_iota(jnp.int32, (TILE, HALF), 1)
    mask = jnp.where((key <= query) & (key >= starts), 0.0, NEG)
    return jnp.concatenate([mask, mask], axis=1)


def in_pairs(first, last, step):
    count = jnp.maximum(last - first, 0)

    def two(i, _):
        step(first + 2 * i, 2)
        return 0

    lax.fori_loop(0, lax.div(count, 2), two, 0)

    @pl.when(lax.rem(count, 2) == 1)
    def _():
        step(last - 1, 1)


def block_of(own_ref, peer_ref, place, tile):
    pair = lax.div(tile, 2)
    own = lax.rem(tile, 2) == lax.rem(place, 2)
    return jnp.where(own, own_ref[pair], peer_ref[pair])


def positions(place):
    return (place * 2 * HALF, 63 * HALF - place * 2 * HALF)


def forward_kernel(place_ref, query_ref, own_ref, peer_ref, starts_ref, attended_ref, out_ref, log_ref, kx, vt, qt, acc, high):
    subs = qt.shape[2] // LANES
    chunk_pos = positions(place_ref[0])

    def prepare(tile, _):
        rows = pl.ds(pl.multiple_of(tile * TILE, TILE), TILE)
        block = block_of(own_ref, peer_ref, place_ref[0], tile)
        kx[rows, :] = with_ones(block[:, :DH])
        vt[:DH, rows] = block[:, DH:].T
        return 0

    lax.fori_loop(0, 2 * own_ref.shape[0], prepare, 0, unroll=4)
    vt[DH:, :] = jnp.ones_like(vt[DH:, :])

    def chunk(c, _):
        first = jnp.where(c == 0, chunk_pos[0], chunk_pos[1])
        diag = lax.div(first, TILE)
        lines = pl.ds(pl.multiple_of(c * HALF, HALF), HALF)
        starts = starts_ref[c]
        wide = jnp.concatenate([starts, starts], axis=1)
        spans = [slice(s * LANES, (s + 1) * LANES) for s in range(subs)]
        for s, cols in enumerate(spans):
            pair = query_ref[lines, s * 2 * DH : (s + 1) * 2 * DH].T
            qt[c, :DH, cols] = jnp.concatenate([pair[:DH], pair[DH:]], axis=1)
            qt[c, DH:, cols] = jnp.zeros_like(qt[c, DH:, cols])

        def rows_of(tile, count=1):
            return pl.ds(pl.multiple_of(tile * TILE, TILE), count * TILE)

        def scores(tile, count=1):
            return [mm(kx[rows_of(tile, count), :], qt[c, :, cols]) for cols in spans]

        def gather(tile, probs, fresh=False, count=1):
            rows = rows_of(tile, count)
            for cols, prob in zip(spans, probs):
                part = mm(vt[:, rows], prob)
                if fresh:
                    acc[c, :, cols] = part
                else:
                    acc[c, :, cols] += part

        def exps(values):
            return [jnp.exp(v).astype(jnp.bfloat16) for v in values]

        def set_shift(used):
            for cols in spans:
                if used:
                    block = pieces(jnp.where(wide <= TILE, high[c, :1, cols], -NEG), LANES)
                else:
                    block = jnp.zeros((16, LANES), jnp.bfloat16)
                qt[c, DH : DH + 16, cols] = block

        def sweep(again):
            mask = mask_of(diag, first, starts)
            values = [v + mask for v in scores(diag)]
            if again:
                tops = [high[c, :1, cols] for cols in spans]
            else:
                tops = [jnp.max(v, axis=0, keepdims=True) for v in values]
                for cols, top in zip(spans, tops):
                    high[c, :1, cols] = top
            gather(diag, exps([v - top for v, top in zip(values, tops)]), fresh=True)

            @pl.when(diag > 0)
            def _():
                set_shift(True)
                mask = mask_of(0, first, starts)
                gather(0, exps([v + mask for v in scores(0)]))
                in_pairs(1, diag, lambda tile, count: gather(tile, exps(scores(tile, count)), count=count))

        sweep(False)

        @pl.when(jnp.logical_not(jnp.max(acc[c, DH : DH + 1, :]) < 1e30))
        def _():
            set_shift(False)

            def raise_to(values):
                for cols, v in zip(spans, values):
                    high[c, :1, cols] = jnp.maximum(high[c, :1, cols], jnp.max(v, axis=0, keepdims=True))

            @pl.when(diag > 0)
            def _():
                mask = mask_of(0, first, starts)
                raise_to([v + mask for v in scores(0)])

                def step(tile, _):
                    raise_to([jnp.where(wide <= TILE, v, NEG) for v in scores(tile)])
                    return 0

                lax.fori_loop(1, diag, step, 0)

            sweep(True)

        for s, cols in enumerate(spans):
            total = acc[c, DH : DH + 1, cols]
            result = acc[c, :DH, cols] / total
            out_ref[c, :, cols] = result
            log_ref[c, :, cols] = high[c, :1, cols] + jnp.log(total)
            stacked = jnp.concatenate([result[:, :HALF], result[:, HALF:]], axis=0)
            attended_ref[lines, s * 2 * DH : (s + 1) * 2 * DH] = stacked.astype(jnp.bfloat16).T
        return 0

    lax.fori_loop(0, 2, chunk, 0)


def backward_kernel(
    place_ref, query_ref, own_ref, peer_ref, starts_ref, grad_ref, out_ref, log_ref,
    dquery_ref, mine_ref, theirs_ref, kx, vx, kt, qt, gt, wq, wg, dq, dkv,
):
    subs = qt.shape[2] // LANES
    place = place_ref[0]
    chunk_pos = positions(place)

    def prepare(tile, _):
        rows = pl.ds(pl.multiple_of(tile * TILE, TILE), TILE)
        block = block_of(own_ref, peer_ref, place, tile)
        kx[rows, :] = with_ones(block[:, :DH])
        vx[rows, :] = with_ones(block[:, DH:])
        kt[:, rows] = block[:, :DH].T
        return 0

    lax.fori_loop(0, 2 * own_ref.shape[0], prepare, 0, unroll=4)
    dkv[...] = jnp.zeros_like(dkv)

    def chunk(c, _):
        first = jnp.where(c == 0, chunk_pos[0], chunk_pos[1])
        diag = lax.div(first, TILE)
        lines = pl.ds(pl.multiple_of(c * HALF, HALF), HALF)
        starts = jnp.concatenate([starts_ref[c], starts_ref[c]], axis=1)
        empty = jnp.zeros((HALF, DH), jnp.bfloat16)
        for s in range(subs):
            cols = slice(s * LANES, (s + 1) * LANES)
            q2 = query_ref[lines, s * 2 * DH : (s + 1) * 2 * DH]
            g2 = grad_ref[lines, s * 2 * DH : (s + 1) * 2 * DH]
            q2t, g2t = q2.T, g2.T
            qt[c, :DH, cols] = jnp.concatenate([q2t[:DH], q2t[DH:]], axis=1)
            grad_t = jnp.concatenate([g2t[:DH], g2t[DH:]], axis=1)
            gt[c, :DH, cols] = grad_t
            qt[c, DH:, cols] = jnp.zeros_like(qt[c, DH:, cols])
            gt[c, DH + 16 :, cols] = jnp.zeros_like(gt[c, DH + 16 :, cols])
            delta = jnp.sum(grad_t.astype(jnp.float32) * out_ref[c, :, cols], axis=0, keepdims=True)
            gt[c, DH : DH + 16, cols] = pieces(delta, LANES)
            for h in range(2):
                rows = slice(h * HALF, (h + 1) * HALF)
                wq[c, s, rows, :] = jnp.concatenate([q2[:, h * DH : (h + 1) * DH], empty], axis=1)
                wg[c, s, rows, :] = jnp.concatenate([empty, g2[:, h * DH : (h + 1) * DH]], axis=1)

        def add(tile, mask=None, logs=None, fresh=False, count=1):
            rows = pl.ds(pl.multiple_of(tile * TILE, TILE), count * TILE)
            total = jnp.zeros((count * TILE, 2 * DH), jnp.float32)
            for base in range(0, subs, 3):
                group = range(base, base + 3)
                spans = [slice(s * LANES, (s + 1) * LANES) for s in group]
                sts = [mm(kx[rows, :], qt[c, :, cols]) for cols in spans]
                dps = [mm(vx[rows, :], gt[c, :, cols]) for cols in spans]
                if mask is not None:
                    sts = [st + mask for st in sts]
                if logs is not None:
                    sts = [st - log_ref[c, :, cols] for st, cols in zip(sts, spans)]
                probs = [jnp.exp(st) for st in sts]
                dss = [(p * dp).astype(jnp.bfloat16) for p, dp in zip(probs, dps)]
                lows = [p.astype(jnp.bfloat16) for p in probs]
                for s, ds, low in zip(group, dss, lows):
                    total = total + (mm(ds, wq[c, s]) + mm(low, wg[c, s]))
                for cols, ds in zip(spans, dss):
                    part = mm(kt[:, rows], ds)
                    if fresh:
                        dq[c, :, cols] = part
                    else:
                        dq[c, :, cols] += part
            dkv[rows, :] += total

        add(diag, mask_of(diag, first, starts_ref[c]), log_ref, fresh=True)

        @pl.when(diag > 0)
        def _():
            for s in range(subs):
                cols = slice(s * LANES, (s + 1) * LANES)
                qt[c, DH : DH + 16, cols] = pieces(jnp.where(starts <= TILE, log_ref[c, :, cols], -NEG), LANES)
            add(0, mask_of(0, first, starts_ref[c]))

            in_pairs(1, diag, lambda tile, count: add(tile, count=count))

        for s in range(subs):
            cols = slice(s * LANES, (s + 1) * LANES)
            result = dq[c, :, cols] * 0.125
            stacked = jnp.concatenate([result[:, :HALF], result[:, HALF:]], axis=0)
            dquery_ref[lines, s * 2 * DH : (s + 1) * 2 * DH] = stacked.astype(jnp.bfloat16).T
        return 0

    lax.fori_loop(0, 2, chunk, 0)

    core = lax.rem(place, 2)

    def give(pair, _):
        for ref, owner in ((mine_ref, 2 * pair + core), (theirs_ref, 2 * pair + 1 - core)):
            for c, pos in enumerate(positions(owner)):
                rows = pl.ds(pl.multiple_of(pos, HALF), HALF)
                ref[pair, c * HALF : (c + 1) * HALF, :] = dkv[rows, :].astype(jnp.bfloat16)
        return 0

    lax.fori_loop(0, mine_ref.shape[0], give, 0)


VM = pl.BlockSpec(memory_space=pltpu.VMEM)
SM = pl.BlockSpec(memory_space=pltpu.SMEM)


def attend(place, query8, own, peer, starts):
    rows, width = query8.shape
    window = 2 * own.shape[0] * own.shape[1]
    lanes = (width // DH) * HALF
    return pl.pallas_call(
        forward_kernel,
        out_shape=(
            jax.ShapeDtypeStruct((rows, width), jnp.bfloat16),
            jax.ShapeDtypeStruct((2, DH, lanes), jnp.float32),
            jax.ShapeDtypeStruct((2, 1, lanes), jnp.float32),
        ),
        in_specs=[SM] + [VM] * 4,
        out_specs=(VM, VM, VM),
        scratch_shapes=[
            pltpu.VMEM((window, HALF), jnp.bfloat16),
            pltpu.VMEM((DH + 16, window), jnp.bfloat16),
            pltpu.VMEM((2, HALF, lanes), jnp.bfloat16),
            pltpu.VMEM((2, DH + 16, lanes), jnp.float32),
            pltpu.VMEM((2, 8, lanes), jnp.float32),
        ],
        compiler_params=pltpu.CompilerParams(vmem_limit_bytes=16 * 2**20),
        cost_estimate=pl.CostEstimate(flops=25 * 10**9, bytes_accessed=8 * 2**20, transcendentals=13 * 10**6),
        name="attend",
    )(place, query8, own, peer, starts)


def attend_back(place, query8, own, peer, starts, grad, out, logs):
    rows, width = query8.shape
    window = 2 * own.shape[0] * own.shape[1]
    lanes = (width // DH) * HALF
    subs = lanes // LANES
    return pl.pallas_call(
        backward_kernel,
        out_shape=(
            jax.ShapeDtypeStruct((rows, width), jnp.bfloat16),
            jax.ShapeDtypeStruct((window // (4 * HALF), 2 * HALF, 2 * DH), jnp.bfloat16),
            jax.ShapeDtypeStruct((window // (4 * HALF), 2 * HALF, 2 * DH), jnp.bfloat16),
        ),
        in_specs=[SM] + [VM] * 7,
        out_specs=(VM, VM, VM),
        scratch_shapes=[
            pltpu.VMEM((window, HALF), jnp.bfloat16),
            pltpu.VMEM((window, HALF), jnp.bfloat16),
            pltpu.VMEM((DH, window), jnp.bfloat16),
            pltpu.VMEM((2, HALF, lanes), jnp.bfloat16),
            pltpu.VMEM((2, HALF, lanes), jnp.bfloat16),
            pltpu.VMEM((2, subs, LANES, HALF), jnp.bfloat16),
            pltpu.VMEM((2, subs, LANES, HALF), jnp.bfloat16),
            pltpu.VMEM((2, DH, lanes), jnp.float32),
            pltpu.VMEM((window, HALF), jnp.float32),
        ],
        compiler_params=pltpu.CompilerParams(vmem_limit_bytes=26 * 2**20),
        cost_estimate=pl.CostEstimate(flops=45 * 10**9, bytes_accessed=12 * 2**20, transcendentals=13 * 10**6),
        name="attend_back",
    )(place, query8, own, peer, starts, grad, out, logs)


EPS = 1e-05
CUBE = 0.044715
VECTOR_ROWS = 64
BLOCKS = 6
ROOT = math.sqrt(2.0 / math.pi)


def mm_cols(left, right):
    return lax.dot_general(left, right, (((1,), (1,)), ((), ())), preferred_element_type=jnp.float32)


def statistics(values):
    center = values - jnp.mean(values, axis=-1, keepdims=True)
    spread = jnp.mean(center * center, axis=-1, keepdims=True)
    scale = lax.rsqrt(spread + EPS)
    return center * scale, scale


def residual_kernel(
    attended_ref, tokens_ref, mine_ref, theirs_ref, bias_ref, gain_ref, shift_ref, middle_ref, normed_ref
):
    width = mine_ref.shape[0]
    rows = mm(attended_ref[:, :width], mine_ref[...]) + mm(attended_ref[:, width:], theirs_ref[...])
    middle = tokens_ref[...].astype(jnp.float32) + rows + bias_ref[...]
    middle_ref[...] = middle
    normal, _ = statistics(middle)
    normed_ref[...] = (normal * gain_ref[...] + shift_ref[...]).astype(jnp.bfloat16)


def own_kernel(tokens_ref, gain_ref, shift_ref, weight_ref, bias_ref, blocks_ref):
    normal, _ = statistics(tokens_ref[...].astype(jnp.float32))
    normed = (normal * gain_ref[...] + shift_ref[...]).astype(jnp.bfloat16)
    bias = jnp.concatenate([jnp.zeros_like(bias_ref[...]), bias_ref[...]], axis=1)
    keyval = (mm(normed, weight_ref[...]) + bias).astype(jnp.bfloat16)
    for i in range(blocks_ref.shape[0]):
        blocks_ref[i] = keyval


def query_kernel(
    own_ref, half_ref, gain_ref, shift_ref, mine_ref, theirs_ref, mine_bias_ref, theirs_bias_ref,
    tokens_ref, normed_ref, query_ref,
):
    half, width = half_ref.shape[0], mine_ref.shape[1]
    tokens_ref[:half, :] = own_ref[:half, :]
    tokens_ref[half:, :] = half_ref[...]
    normal, _ = statistics(tokens_ref[...].astype(jnp.float32))
    normed = (normal * gain_ref[...] + shift_ref[...]).astype(jnp.bfloat16)
    normed_ref[...] = normed
    mine = (mm(normed, mine_ref[...]) + mine_bias_ref[...]).astype(jnp.bfloat16)
    theirs = (mm(normed, theirs_ref[...]) + theirs_bias_ref[...]).astype(jnp.bfloat16)
    query_ref[:, :width] = mine * jnp.bfloat16(0.125)
    query_ref[:, width:] = theirs * jnp.bfloat16(0.125)


def mlp_kernel(
    own_ref, peer_ref, own_grad_ref, peer_grad_ref, expand_ref, bias_ref, contract_ref,
    contract_part_ref, expand_part_ref, bias_part_ref, own_out_ref, peer_out_ref, own_back_ref, peer_back_ref,
    both, turned, grads, acts_all, grad_all,
):
    rows = own_ref.shape[0]
    hidden = expand_ref.shape[1]
    block = hidden // BLOCKS
    both[:rows, :] = own_ref[...]
    both[rows:, :] = peer_ref[...]
    grads[:rows, :] = own_grad_ref[...]
    grads[rows:, :] = peer_grad_ref[...]
    spans = [slice(j * block, (j + 1) * block) for j in range(BLOCKS)]

    def products(cols):
        return mm(both[...], expand_ref[:, cols]), mm_cols(grads[...], contract_ref[cols, :])

    def activate(cols, inner, acts_grad):
        inner = inner + bias_ref[:, cols]
        square = inner * inner
        tanh = jnp.tanh(inner * (ROOT + ROOT * CUBE * square))
        half = 0.5 + 0.5 * tanh
        acts_all[:, cols] = (inner * half).astype(jnp.bfloat16)
        slope = half + inner * (0.5 - 0.5 * tanh * tanh) * (ROOT + 3.0 * ROOT * CUBE * square)
        grad = (acts_grad * slope).astype(jnp.bfloat16)
        grad_all[:, cols] = grad
        bias_part_ref[:, cols] = jnp.sum(grad.astype(jnp.float32), axis=0, keepdims=True)

    def weights(cols):
        contract_part_ref[cols, :] = mm(acts_all[:, cols].T, grads[...]).astype(jnp.bfloat16)
        expand_part_ref[:, cols] = mm(turned[...], grad_all[:, cols]).astype(jnp.bfloat16)

    turned[...] = both[...].T
    held = products(spans[0])
    for j, cols in enumerate(spans):
        later = products(spans[j + 1]) if j + 1 < BLOCKS else None
        activate(cols, *held)
        held = later
    for cols in spans:
        weights(cols)
    out = mm(acts_all[...], contract_ref[...])
    own_out_ref[...] = out[:rows, :]
    peer_out_ref[...] = out[rows:, :].astype(jnp.bfloat16)
    back = mm_cols(grad_all[...], expand_ref[...])
    own_back_ref[...] = back[:rows, :]
    peer_back_ref[...] = back[rows:, :].astype(jnp.bfloat16)


def widen_kernel(contract_ref, expand_ref, contract_out_ref, expand_out_ref):
    contract_out_ref[...] = contract_ref[...].astype(jnp.float32)
    expand_out_ref[...] = expand_ref[...].astype(jnp.float32)


def residual_back_kernel(
    back_ref, peer_back_ref, grad_ref, middle_ref, gain_ref, mine_ref, theirs_ref,
    middle_grad_ref, low_ref, attended_grad_ref, sums_ref,
):
    width = mine_ref.shape[0]
    back = back_ref[...] + peer_back_ref[...].astype(jnp.float32)
    grad = grad_ref[...].astype(jnp.float32)
    normal, scale = statistics(middle_ref[...])
    weighted = back * gain_ref[...]
    mean = jnp.mean(weighted, axis=-1, keepdims=True)
    along = jnp.mean(weighted * normal, axis=-1, keepdims=True)
    middle_grad = grad + scale * (weighted - mean - normal * along)
    middle_grad_ref[...] = middle_grad
    lowered = middle_grad.astype(jnp.bfloat16)
    low_ref[...] = lowered
    attended_grad_ref[:, :width] = mm_cols(lowered, mine_ref[...]).astype(jnp.bfloat16)
    attended_grad_ref[:, width:] = mm_cols(lowered, theirs_ref[...]).astype(jnp.bfloat16)
    sums_ref[0:1, :] = jnp.sum(middle_grad, axis=0, keepdims=True)
    sums_ref[1:2, :] = jnp.sum(back * normal, axis=0, keepdims=True)
    sums_ref[2:3, :] = jnp.sum(back, axis=0, keepdims=True)
    sums_ref[3:4, :] = jnp.sum(grad, axis=0, keepdims=True)


def query_back_kernel(
    grad_ref, normed_ref, attended_ref, low_ref, mine_ref, theirs_ref,
    normed_grad_ref, mine_part_ref, theirs_part_ref, mine_out_ref, theirs_out_ref, bias_ref,
):
    width = mine_ref.shape[1]
    normed = normed_ref[...].T
    attended = attended_ref[...].T
    mine, theirs = grad_ref[:, :width], grad_ref[:, width:]
    normed_grad_ref[...] = mm_cols(mine, mine_ref[...]) + mm_cols(theirs, theirs_ref[...])
    theirs_part_ref[...] = mm(normed, theirs).astype(jnp.bfloat16)
    theirs_out_ref[...] = mm(attended[width:], low_ref[...]).astype(jnp.bfloat16)
    mine_part_ref[...] = mm(normed, mine)
    mine_out_ref[...] = mm(attended[:width], low_ref[...])
    bias_ref[...] = jnp.sum(grad_ref[...].astype(jnp.float32), axis=0, keepdims=True)


def token_back_kernel(
    arrived_ref, normed_grad_ref, weight_ref, tokens_ref, gain_ref, normed_ref, middle_grad_ref,
    middle_sums_ref, query_bias_ref, expand_bias_ref,
    tokens_grad_ref, half_ref, sent_ref, rows_ref,
):
    grad = arrived_ref[0].astype(jnp.float32)
    for i in range(1, arrived_ref.shape[0]):
        grad = grad + arrived_ref[i].astype(jnp.float32)
    grad = grad.astype(jnp.bfloat16)
    back = normed_grad_ref[...] + mm_cols(grad, weight_ref[...])
    normal, scale = statistics(tokens_ref[...].astype(jnp.float32))
    weighted = back * gain_ref[...]
    mean = jnp.mean(weighted, axis=-1, keepdims=True)
    along = jnp.mean(weighted * normal, axis=-1, keepdims=True)
    tokens_grad = middle_grad_ref[...] + scale * (weighted - mean - normal * along)
    half = half_ref.shape[0]
    tokens_grad_ref[...] = tokens_grad[:half]
    half_ref[...] = tokens_grad[half:].astype(jnp.bfloat16)

    place = 0

    def put(values):
        nonlocal place
        depth = values.shape[0]
        sent_ref[place : place + depth, :] = values.astype(jnp.bfloat16)
        place += depth

    put(mm(normed_ref[...].T, grad))
    vectors = [middle_sums_ref[i : i + 1, :] for i in range(4)]
    vectors += [jnp.sum(back * normal, axis=0, keepdims=True), jnp.sum(back, axis=0, keepdims=True)]
    vectors += [query_bias_ref[...], jnp.sum(grad.astype(jnp.float32), axis=0, keepdims=True), expand_bias_ref[...]]
    rows_ref[...] = jnp.zeros_like(rows_ref)
    row = 0
    for vector in vectors:
        for col in range(0, vector.shape[1], HALF):
            rows_ref[row : row + 1, :] = vector[:, col : col + HALF]
            row += 1
    rows = rows_ref[...]
    high = rows.astype(jnp.bfloat16)
    put(high)
    put(rows - high.astype(jnp.float32))
    sent_ref[place:, :] = jnp.zeros_like(sent_ref[place:, :])


def pack_kernel(
    win_ref, query_ref, peer_query_ref, out_ref, peer_out_ref, own_ref, first_ref, second_ref, third_ref, packed
):
    place = 0
    for ref, peer in ((query_ref, peer_query_ref), (out_ref, peer_out_ref)):
        depth = ref.shape[0]
        for col in range(0, ref.shape[1], HALF):
            span = slice(col, col + HALF)
            packed[place : place + depth, :] = ref[:, span] + peer[:, span].astype(jnp.float32)
            place += depth
    depth = own_ref.shape[0]
    count = place // depth
    for shift, ref in enumerate((own_ref, first_ref, second_ref, third_ref)):
        to = lax.rem(win_ref[0] + shift, count)
        rows = pl.ds(pl.multiple_of(to * depth, HALF), depth)
        ref[...] = packed[rows, :].astype(ref.dtype)


def unpack_kernel(weights_ref, rest_ref, query_ref, out_ref, keyval_ref, rows_ref):
    place = 0
    for ref in (query_ref, out_ref):
        depth = ref.shape[0]
        for col in range(0, ref.shape[1], HALF):
            ref[:, col : col + HALF] = weights_ref[place : place + depth, :].astype(jnp.float32)
            place += depth
    place = keyval_ref.shape[0]
    keyval_ref[...] = rest_ref[:place, :].astype(jnp.float32)
    depth = rows_ref.shape[0]
    high = rest_ref[place : place + depth, :].astype(jnp.float32)
    rows_ref[...] = high + rest_ref[place + depth : place + 2 * depth, :].astype(jnp.float32)


def like(*shape, dtype=jnp.float32):
    return jax.ShapeDtypeStruct(shape, dtype)


def run(kernel, outs, scratch, limit, flops, name, *args):
    return pl.pallas_call(
        kernel,
        out_shape=outs,
        in_specs=[VM] * len(args),
        out_specs=tuple(VM for _ in outs),
        scratch_shapes=scratch,
        compiler_params=pltpu.CompilerParams(vmem_limit_bytes=limit * 2**20),
        cost_estimate=pl.CostEstimate(flops=flops, bytes_accessed=2**20, transcendentals=0),
        name=name,
    )(*args)


def residual(attended, tokens, pair, bias, gain, shift):
    outs = (like(*tokens.shape), like(*tokens.shape, dtype=jnp.bfloat16))
    rows = (bias[None], gain[None], shift[None])
    return run(residual_kernel, outs, [], 12, 10**9, "residual", attended, tokens, *pair, *rows)


def own_keyval_blocks(tokens, gain, shift, weight, bias, count):
    outs = (like(count, tokens.shape[0], weight.shape[1], dtype=jnp.bfloat16),)
    return run(own_kernel, outs, [], 8, 10**8, "own_keyval", tokens, gain[None], shift[None], weight, bias[None])[0]


def query_rows(own, half, gain, shift, pair, biases):
    low16 = like(*own.shape, dtype=jnp.bfloat16)
    rows = (gain[None], shift[None])
    outs = (low16, low16, low16)
    return run(
        query_kernel, outs, [], 12, 3 * 10**10, "query_rows", own, half, *rows, *pair, biases[0][None], biases[1][None]
    )


def mlp(own, peer, own_grad, peer_grad, expand, bias, contract):
    rows, features = own.shape
    hidden = expand.shape[1]
    b16 = jnp.bfloat16
    outs = (
        like(hidden, features, dtype=b16),
        like(features, hidden, dtype=b16),
        like(1, hidden),
        like(rows, features),
        like(rows, features, dtype=b16),
        like(rows, features),
        like(rows, features, dtype=b16),
    )
    scratch = [
        pltpu.VMEM((2 * rows, features), b16),
        pltpu.VMEM((features, 2 * rows), b16),
        pltpu.VMEM((2 * rows, features), b16),
        pltpu.VMEM((2 * rows, hidden), b16),
        pltpu.VMEM((2 * rows, hidden), b16),
    ]
    return run(
        mlp_kernel, outs, scratch, 32, 10**10, "mlp", own, peer, own_grad, peer_grad, expand, bias[None], contract
    )


def widen(contract, expand):
    steps = 2

    def spec(array):
        return pl.BlockSpec((array.shape[0] // steps, array.shape[1]), lambda i: (i, 0))

    return pl.pallas_call(
        widen_kernel,
        grid=(steps,),
        out_shape=(like(*contract.shape), like(*expand.shape)),
        in_specs=[spec(contract), spec(expand)],
        out_specs=(spec(contract), spec(expand)),
        compiler_params=pltpu.CompilerParams(vmem_limit_bytes=60 * 2**20),
        name="widen",
    )(contract, expand)


def residual_back(back, peer_back, grad, middle, gain, pair):
    rows, features = grad.shape
    b16 = jnp.bfloat16
    outs = (like(rows, features), like(rows, features, dtype=b16), like(rows, features, dtype=b16), like(8, features))
    return run(
        residual_back_kernel, outs, [], 12, 10**9, "residual_back", back, peer_back, grad, middle, gain[None], *pair
    )


SWAP = ((0, 1), (1, 0))


def query_back(grad, normed, attended, lowered, pair):
    rows, features = grad.shape
    width = pair[0].shape[1]
    b16 = jnp.bfloat16
    outs = (
        like(rows, features),
        like(features, width),
        like(features, width, dtype=b16),
        like(width, features),
        like(width, features, dtype=b16),
        like(1, features),
    )
    return run(query_back_kernel, outs, [], 16, 10**10, "query_back", grad, normed, attended, lowered, *pair)


def token_back(ranks, arrived, normed_grad, weight, tokens, gain, normed, middle_grad, vectors):
    rows, features = normed.shape
    depth = weight.shape[0] + 2 * VECTOR_ROWS
    depth += -depth % (16 * ranks)
    outs = (like(rows // 2, features), like(rows // 2, features, dtype=jnp.bfloat16), like(depth, HALF, dtype=jnp.bfloat16))
    return run(
        token_back_kernel, outs, [pltpu.VMEM((VECTOR_ROWS, HALF), jnp.float32)], 12, 10**9, "token_back",
        arrived, normed_grad, weight, tokens, gain[None], normed, middle_grad, *vectors,
    )


def pack(win, query_part, peer_query, out_part, peer_out):
    depth = (query_part.size + out_part.size) // HALF // 4
    outs = (like(depth, HALF), *(like(depth, HALF, dtype=jnp.bfloat16) for _ in range(3)))
    return pl.pallas_call(
        pack_kernel,
        out_shape=outs,
        in_specs=[SM] + [VM] * 4,
        out_specs=(VM,) * 4,
        scratch_shapes=[pltpu.VMEM((4 * depth, HALF), jnp.float32)],
        compiler_params=pltpu.CompilerParams(vmem_limit_bytes=16 * 2**20),
        name="pack",
    )(win, query_part, peer_query, out_part, peer_out)


def unpack(weights, rest, query_shape, out_shape, keyval_shape):
    outs = (like(*query_shape), like(*out_shape), like(*keyval_shape), like(VECTOR_ROWS, HALF))
    return run(unpack_kernel, outs, [], 12, 10**8, "unpack", weights, rest)


def low(value):
    return value.astype(jnp.bfloat16)


def swapped(value):
    return lax.ppermute(value, "heads", SWAP)


def opposite(value):
    count = lax.axis_size(("seq", "heads"))
    return lax.ppermute(value, ("seq", "heads"), [(i, count - 1 - i) for i in range(count)])


def exchanged(value):
    half = value.shape[0] // 2
    return jnp.concatenate([value[:half], opposite(value[half:])], axis=0)


def spread_out(blocks, axis):
    return lax.all_to_all(blocks, axis, split_axis=0, concat_axis=0, tiled=True)


def copies(value, axis):
    return spread_out(jnp.broadcast_to(value[None], (lax.axis_size(axis), *value.shape)), axis)


def per_device(
    tokens,
    first_gain,
    first_shift,
    query_weight,
    query_bias,
    keyval_weight,
    value_bias,
    out_weight,
    out_bias,
    second_gain,
    second_shift,
    expand_weight,
    expand_bias,
    contract_weight,
    contract_bias,
    cotangent,
    lengths,
):
    f32 = jnp.float32
    place = lax.axis_index(("seq", "heads"))
    places = place.astype(jnp.int32).reshape(1)
    ranks = lax.axis_size(("win", "seq"))

    received = opposite(jnp.concatenate([tokens[0, HALF:], cotangent[0, HALF:]]))
    tokens_half = received[:HALF]
    grad_low = jnp.concatenate([cotangent[0, :HALF], received[HALF:]])
    own_blocks = own_keyval_blocks(
        tokens[0], first_gain, first_shift, keyval_weight, value_bias, lax.axis_size("seq")
    )
    own_blocks = spread_out(own_blocks, "seq")
    query_pair = (query_weight, swapped(query_weight))
    out_pair = (out_weight, swapped(out_weight))
    query_biases = (query_bias, swapped(query_bias))

    bounds = jnp.cumsum(lengths[0])
    first = jnp.stack(positions(place.astype(jnp.int32)))
    position = first[:, None] + jnp.arange(HALF, dtype=jnp.int32)[None, :]
    starts = jnp.max(jnp.where(bounds[None, None, :] <= position[:, :, None], bounds, 0), axis=2)
    starts = starts.astype(jnp.int32).reshape(2, 1, HALF)

    tokens_low, normed_low, query8 = query_rows(
        tokens[0], tokens_half, first_gain, first_shift, query_pair, query_biases
    )
    own_blocks, query8 = lax.optimization_barrier((own_blocks, query8))
    peer_blocks = swapped(own_blocks)
    attended, out, logs = attend(places, query8, own_blocks, peer_blocks, starts)
    width = query_bias.shape[0]
    middle, normed2_low = residual(attended, tokens_low, out_pair, out_bias, second_gain, second_shift)
    peer_grad_low = swapped(grad_low)
    contract_part, expand_part, expand_bias_part, out_rows, peer_out, back_rows, peer_back = mlp(
        normed2_low, swapped(normed2_low), grad_low, peer_grad_low, expand_weight, expand_bias, contract_weight
    )
    contract_total, expand_total = lax.psum((contract_part, expand_part), ("win", "seq"))
    middle_grad, middle_low, attended_grad, middle_sums = residual_back(
        back_rows, swapped(peer_back), grad_low, middle, second_gain, out_pair
    )

    def rest():
        query_grad, mine, theirs = attend_back(
            places, query8, own_blocks, peer_blocks, starts, attended_grad, out, logs
        )
        mlp_out = out_rows + swapped(peer_out).astype(f32)
        block_out = exchanged(low(middle + mlp_out + contract_bias))
        pair_grad = low(mine.astype(f32) + swapped(theirs).astype(f32))
        arrived = spread_out(pair_grad, "seq")
        from_query, query_part, query_sent, out_part, out_sent, query_bias_part = query_back(
            query_grad, normed_low, attended, middle_low, query_pair
        )
        core = lax.axis_index("heads")
        turned_bias = jnp.concatenate([query_bias_part[:, width:], query_bias_part[:, :width]], axis=1)
        query_bias_part = jnp.where(core == 0, query_bias_part, turned_bias)
        wins, seqs = lax.axis_size("win"), lax.axis_size("seq")
        win = lax.axis_index("win").astype(jnp.int32)
        kept, *given = pack(win.reshape(1), query_part, swapped(query_sent), out_part, swapped(out_sent))
        taken = [
            lax.ppermute(g, "win", [(i, (i + shift) % wins) for i in range(wins)]) for shift, g in enumerate(given, 1)
        ]
        tokens_grad, half, sent = token_back(
            ranks, arrived, from_query, keyval_weight, tokens_low, first_gain, normed_low, middle_grad,
            (middle_sums, query_bias_part, expand_bias_part),
        )
        tokens_grad = jnp.concatenate([tokens_grad, opposite(half).astype(f32)], axis=0)

        sent, taken = lax.optimization_barrier((sent, taken))
        rest = spread_out(sent.reshape(wins, -1, HALF), "win")
        rest = low(jnp.sum(rest.astype(f32), axis=0)).reshape(seqs, -1, HALF)
        weights = low(kept + sum(t.astype(f32) for t in taken)).reshape(seqs, -1, HALF)
        depth = weights.shape[1]
        summed = jnp.sum(spread_out(jnp.concatenate([weights, rest], axis=1), "seq").astype(f32), axis=0)
        rest = summed[depth:]
        features = first_gain.shape[0]
        row = lax.axis_index(("win", "seq")) * rest.shape[0] + jnp.arange(rest.shape[0])[:, None]
        vectors = keyval_weight.shape[0]
        common = 7 * features // HALF + 1
        shared = row < vectors + common
        shared = shared | ((row >= vectors + VECTOR_ROWS) & (row < vectors + VECTOR_ROWS + common))
        rest = rest + jnp.where(shared, swapped(rest), 0.0)
        full = low(jnp.concatenate([summed[:depth], rest]))
        full = copies(copies(full, "seq"), "win")
        query_total, out_total, keyval_total, rows = unpack(
            full[:, :, :depth].reshape(-1, HALF),
            full[:, :, depth:].reshape(-1, HALF),
            query_weight.shape,
            out_weight.shape,
            keyval_weight.shape,
        )
        rows = rows.reshape(-1)
        sizes = [features] * 7 + [HALF, expand_bias.shape[0]]
        totals = []
        for size in sizes:
            totals.append(rows[:size])
            rows = rows[size:]
        query_bias_total = jnp.where(core == 0, totals[6][:width], totals[6][width:])
        return (
            block_out[None],
            tokens_grad[None],
            totals[4],
            totals[5],
            query_total,
            query_bias_total,
            keyval_total,
            totals[7][DH:],
            out_total,
            totals[0],
            totals[1],
            totals[2],
            totals[8],
            totals[3],
        )

    shapes = jax.eval_shape(rest)

    def nothing():
        return jax.tree.map(lambda s: jnp.zeros(s.shape, s.dtype), shapes)

    outs = lax.cond(lengths[0, 0] > 0, rest, nothing)
    contract_total, expand_total = widen(contract_total, expand_total)
    return (
        *outs[:12],
        expand_total,
        outs[12],
        contract_total,
        outs[13],
    )


def solution(mesh):
    return jax.shard_map(
        per_device,
        mesh=mesh,
        in_specs=(
            P("win", ("seq", "heads"), None),
            P(),
            P(),
            P(None, "heads"),
            P("heads"),
            P(),
            P(),
            P("heads", None),
            P(),
            P(),
            P(),
            P(None, "heads"),
            P("heads"),
            P("heads", None),
            P(),
            P("win", ("seq", "heads"), None),
            P("win", None),
        ),
        out_specs=(
            P("win", ("seq", "heads"), None),
            P("win", ("seq", "heads"), None),
            P(),
            P(),
            P(None, "heads"),
            P("heads"),
            P(),
            P(),
            P("heads", None),
            P(),
            P(),
            P(),
            P(None, "heads"),
            P("heads"),
            P("heads", None),
            P(),
        ),
        check_vma=False,
    )
```

profile of v0, /device:TPU:0, one launch (start us, length us, event | category | flops | bytes accessed | tf_op | source)
XLA Modules:
  0.0 254.6 jit_solution(6882041153317229481)
XLA Ops:
  7.2 1.0 slice_bitcast_fusion.10
  8.2 1.1 slice_bitcast_fusion.8
  9.3 5.8 %collective-permute-start.10 = (bf16[256,768]{1,0:T(8,128)(2,1)S(1)}, bf16[256,768]{1,0:T(8,128)(2,1)S(1)}, u32[]{:S(2)}, u32[]{:S(2)}) collective-permute-start(bf16[256,768]{1,0:T(8,128)(2,1)S(1)} %pad_maximum_fusion.2), channel_id=1, source_target_pairs={{0,31},{1,30},{2,29},{3,28},{4,27},{5,26},{6,25},{7,24},{8,23},{9,... | collective-permute-start | bytes 1179656 | tf_op jit(solution)/shard_map/ppermute | solution.py:700
  15.1 0.7 collective-permute-start.11
  15.8 0.7 broadcast_in_dim.76.shift_ref
  16.5 0.7 broadcast_in_dim.75.gain_ref
  17.2 0.6 copy-done.3
  17.9 1.5 own_keyval.1
  19.4 3.7 %all-to-all-start.5 = ((bf16[16,256,128]{2,1,0:T(8,128)(2,1)}), bf16[16,256,128]{2,1,0:T(8,128)(2,1)S(1)}, u32[]{:S(2)}, u32[]{:S(2)}) async-start(bf16[16,256,128]{2,1,0:T(8,128)(2,1)} %own_keyval.1), calls=%async_computation.5 | async-start | bytes 2097152 | tf_op jit(solution)/shard_map/all_to_all | solution.py:709
  23.1 1.5 collective-permute-done.10
  24.7 2.4 query_rows.1
  27.2 15.8 %all-to-all-done.5.own_ref = bf16[16,256,128]{2,1,0:T(8,128)(2,1)S(1)} async-done(((bf16[16,256,128]{2,1,0:T(8,128)(2,1)}), bf16[16,256,128]{2,1,0:T(8,128)(2,1)S(1)}, u32[]{:S(2)}, u32[]{:S(2)}) %all-to-all-start.5) | async-done | bytes 1048608 | tf_op jit(solution)/shard_map/all_to_all | solution.py:709
  44.2 2.2 collective-permute-done.13.peer_ref
  46.4 19.4 %attend.1 = (bf16[256,768]{1,0:T(8,128)(2,1)S(1)}, f32[2,64,1536]{2,1,0:T(8,128)}, f32[2,1,1536]{2,1,0:T(1,128)}) custom-call(s32[1]{0:T(128)} %bitcast.18.place_ref, bf16[256,768]{1,0:T(8,128)(2,1)S(1)} %get-tuple-element.147.query_ref, bf16[16,256,128]{2,1,0:T(8,128)(2,1)S(1)} %all-to-all-done.5.own_ref, ...), custom_call_target="tpu_custom_call" | custom-call | flops 24999999488 | bytes 8388608 | tf_op jit(solution)/shard_map/attend/pallas_call | solution.py:279
  65.9 0.8 residual.1
  66.7 0.6 collective-permute-start.15
  67.4 1.3 collective-permute-done.15.peer_ref
  68.7 8.3 %mlp.1 = (bf16[1536,768]{1,0:T(8,128)(2,1)}, bf16[768,1536]{1,0:T(8,128)(2,1)}, f32[1,1536]{1,0:T(1,128)}, f32[256,768]{1,0:T(8,128)}, bf16[256,768]{1,0:T(8,128...) custom-call(bf16[256,768]{1,0:T(8,128)(2,1)S(1)} %get-tuple-element.151.own_ref, ...), custom_call_target="tpu_custom_call" | custom-call | flops 10000000000 | bytes 1048576 | tf_op jit(solution)/shard_map/mlp/pallas_call | solution.py:559
  77.7 1.2 collective-permute-done.17.peer_back_ref
  78.9 1.8 residual_back.1
  80.8 161.5 %conditional.1 = (bf16[1,256,768]{2,1,0:T(8,128)(2,1)}, f32[1,256,768]{2,1,0:T(8,128)}, f32[768]{0:T(1024)}, f32[768]{0:T(1024)}, f32[768,384]{1,0:T(8,128)}, /*...) conditional(s32[]{:T(128)} %bitcast.17, () %tuple.18, ...), branch_computations={%region_2.3_spmd, %region_3.6_spmd} | conditional | flops 56106414080 | bytes 80093312 | solution.py:852
  80.8 37.5 %attend_back.1 = (bf16[256,768]{1,0:T(8,128)(2,1)S(1)}, bf16[16,256,128]{2,1,0:T(8,128)(2,1)S(1)}, bf16[16,256,128]{2,1,0:T(8,128)(2,1)S(1)}) custom-call(s32[1]{0:T(128)} %get-tuple-element.50.place_ref, bf16[256,768]{1,0:T(8,128)(2,1)S(1)} %get-tuple-element.51.query_ref, bf16[16,256,128]{2,1,0:T(8,128)(2,1)S(1)} %get-tuple-element.52.own_ref, ...), custom_call_target="tpu_custom_call" | custom-call | flops 44999999488 | bytes 12582912 | tf_op jit(solution)/shard_map/cond/branch_1_fun/attend_back/pallas_call | solution.py:306
  118.4 0.7 copy-done.9
  119.6 2.3 collective-permute-done.2
  121.9 1.2 add_convert_fusion
  123.1 3.7 %all-to-all-start = ((bf16[16,256,128]{2,1,0:T(8,128)(2,1)}), bf16[16,256,128]{2,1,0:T(8,128)(2,1)S(1)}, u32[]{:S(2)}, u32[]{:S(2)}) async-start(bf16[16,256,128]{2,1,0:T(8,128)(2,1)} %add_convert_fusion), calls=%async_computation | async-start | bytes 2097152 | tf_op jit(solution)/shard_map/cond/branch_1_fun/all_to_all | solution.py:709
  126.8 1.0 copy-done.10
  127.8 3.6 %query_back.1 = (f32[256,768]{1,0:T(8,128)S(1)}, f32[768,384]{1,0:T(8,128)S(1)}, bf16[768,384]{1,0:T(8,128)(2,1)}, f32[384,768]{1,0:T(8,128)S(1)}, bf16[384,768]{1,0:T(8,128)(2,1)}, /*index=5*/f32[1,768]{1,0:T(1,128)S(1)}) custom-call(bf16[256,768]{1,0:T(8,128)(2,1)S(1)} %copy-done.10, bf16[256,768]{1,0:T(8,128)(2,1)} %get-tuple-element.61.normed_ref, ...), custom_call_target="tpu_custom_call" | custom-call | flops 10000000000 | bytes 1048576 | tf_op jit(solution)/shard_map/cond/branch_1_fun/query_back/pallas_call | solution.py:559
  131.3 0.9 copy-done.7
  132.7 1.8 collective-permute-done.4.peer_query_ref
  134.5 0.8 collective-permute-done.5.peer_out_ref
  135.4 2.4 pack.1
  137.8 0.8 copy-done.1
  138.6 1.6 collective-permute-start.6
  140.2 2.9 %collective-permute-start.7 = (bf16[1152,128]{1,0:T(8,128)(2,1)}, bf16[1152,128]{1,0:T(8,128)(2,1)}, u32[]{:S(2)}, u32[]{:S(2)}) collective-permute-start(bf16[1152,128]{1,0:T(8,128)(2,1)} %get-tuple-element.83), channel_id=1, source_target_pairs={{0,64},{32,96},{64,0},{96,32},{1,65},{33,97},{65,1},{97,33},{2,66}... | collective-permute-start | bytes 884744 | tf_op jit(solution)/shard_map/cond/branch_1_fun/ppermute | solution.py:792
  143.1 1.3 collective-permute-start.8
  144.5 2.0 all-to-all-done.arrived_ref
  146.5 1.1 copy-done.8
  147.6 3.0 %token_back.1 = (f32[128,768]{1,0:T(8,128)S(1)}, bf16[128,768]{1,0:T(8,128)(2,1)S(1)}, bf16[1024,128]{1,0:T(8,128)(2,1)}) custom-call(bf16[16,256,128]{2,1,0:T(8,128)(2,1)S(1)} %all-to-all-done.arrived_ref, f32[256,768]{1,0:T(8,128)S(1)} %copy-done.8, bf16[768,128]{1,0:T(8,128)(2,1)} %get-tuple-element.67.weight_ref, ...), custom_call_target="tpu_custom_call" | custom-call | flops 1000000000 | bytes 1048576 | tf_op jit(solution)/shard_map/cond/branch_1_fun/token_back/pallas_call | solution.py:559
  150.6 6.7 %collective-permute-done.7 = bf16[1152,128]{1,0:T(8,128)(2,1)} collective-permute-done((bf16[1152,128]{1,0:T(8,128)(2,1)}, bf16[1152,128]{1,0:T(8,128)(2,1)}, u32[]{:S(2)}, u32[]{:S(2)}) %collective-permute-start.7) | collective-permute-done | bytes 294944 | tf_op jit(solution)/shard_map/cond/branch_1_fun/ppermute | solution.py:792
  157.3 3.7 %all-to-all-start.1 = ((bf16[4,256,128]{2,1,0:T(8,128)(2,1)}), bf16[4,256,128]{2,1,0:T(8,128)(2,1)S(1)}, u32[]{:S(2)}, u32[]{:S(2)}) async-start(bf16[4,256,128]{2,1,0:T(8,128)(2,1)} %bitcast.4), calls=%async_computation.1 | async-start | bytes 524288 | tf_op jit(solution)/shard_map/cond/branch_1_fun/all_to_all | solution.py:709
  161.0 1.2 add_convert_fusion.2
  162.2 5.5 %all-to-all-done.1 = bf16[4,256,128]{2,1,0:T(8,128)(2,1)S(1)} async-done(((bf16[4,256,128]{2,1,0:T(8,128)(2,1)}), bf16[4,256,128]{2,1,0:T(8,128)(2,1)S(1)}, u32[]{:S(2)}, u32[]{:S(2)}) %all-to-all-start.1) | async-done | bytes 262176 | tf_op jit(solution)/shard_map/cond/branch_1_fun/all_to_all | solution.py:709
  167.8 0.8 pad_maximum_fusion
  168.5 7.0 %all-to-all-start.2 = ((bf16[16,88,128]{2,1,0:T(8,128)(2,1)}), bf16[16,88,128]{2,1,0:T(8,128)(2,1)S(1)}, u32[]{:S(2)}, u32[]{:S(2)}) async-start(bf16[16,88,128]{2,1,0:T(8,128)(2,1)} %pad_maximum_fusion), calls=%async_computation.2 | async-start | bytes 720896 | tf_op jit(solution)/shard_map/cond/branch_1_fun/all_to_all | solution.py:709
  175.5 9.2 %all-to-all-done.2 = bf16[16,88,128]{2,1,0:T(8,128)(2,1)S(1)} async-done(((bf16[16,88,128]{2,1,0:T(8,128)(2,1)}), bf16[16,88,128]{2,1,0:T(8,128)(2,1)S(1)}, u32[]{:S(2)}, u32[]{:S(2)}) %all-to-all-start.2) | async-done | bytes 360480 | tf_op jit(solution)/shard_map/cond/branch_1_fun/all_to_all | solution.py:709
  184.9 1.1 collective-permute-done.9
  186.1 0.8 broadcast_in_dim.34
  186.9 3.5 %all-to-all-start.3 = ((bf16[16,88,128]{2,1,0:T(8,128)(2,1)}), bf16[16,88,128]{2,1,0:T(8,128)(2,1)S(1)}, u32[]{:S(2)}, u32[]{:S(2)}) async-start(bf16[16,88,128]{2,1,0:T(8,128)(2,1)} %broadcast_in_dim.34), calls=%async_computation.3 | async-start | bytes 720896 | tf_op jit(solution)/shard_map/cond/branch_1_fun/all_to_all | solution.py:709
  190.7 10.7 %all-to-all-done.3 = bf16[16,88,128]{2,1,0:T(8,128)(2,1)S(1)} async-done(((bf16[16,88,128]{2,1,0:T(8,128)(2,1)}), bf16[16,88,128]{2,1,0:T(8,128)(2,1)S(1)}, u32[]{:S(2)}, u32[]{:S(2)}) %all-to-all-start.3) | async-done | bytes 360480 | tf_op jit(solution)/shard_map/cond/branch_1_fun/all_to_all | solution.py:709
  201.4 1.3 broadcast_in_dim.35
  202.8 3.5 %all-to-all-start.4 = ((bf16[4,16,88,128]{3,2,1,0:T(8,128)(2,1)}), bf16[4,16,88,128]{3,2,1,0:T(8,128)(2,1)S(1)}, u32[]{:S(2)}, u32[]{:S(2)}) async-start(bf16[4,16,88,128]{3,2,1,0:T(8,128)(2,1)} %broadcast_in_dim.35), calls=%async_computation.4 | async-start | bytes 2883584 | tf_op jit(solution)/shard_map/cond/branch_1_fun/all_to_all | solution.py:709
  206.4 1.5 add_convert_fusion.1
  208.3 4.7 %collective-permute-start.3 = (bf16[128,768]{1,0:T(8,128)(2,1)S(1)}, bf16[128,768]{1,0:T(8,128)(2,1)S(1)}, u32[]{:S(2)}, u32[]{:S(2)}) collective-permute-start(bf16[128,768]{1,0:T(8,128)(2,1)S(1)} %get-tuple-element.75), channel_id=1, source_target_pairs={{0,31},{1,30},{2,29},{3,28},{4,27},{5,26},{6,25},{7,24},{8,23},{9,... | collective-permute-start | bytes 589832 | tf_op jit(solution)/shard_map/cond/branch_1_fun/ppermute | solution.py:700
  213.0 9.2 %collective-permute-done.1 = bf16[128,768]{1,0:T(8,128)(2,1)S(1)} collective-permute-done((bf16[128,768]{1,0:T(8,128)(2,1)S(1)}, bf16[128,768]{1,0:T(8,128)(2,1)S(1)}, u32[]{:S(2)}, u32[]{:S(2)}) %collective-permute-start.1) | collective-permute-done | bytes 196640 | tf_op jit(solution)/shard_map/cond/branch_1_fun/ppermute | solution.py:700
  222.3 0.8 maximum_bitcast_fusion.1
  223.0 7.5 %collective-permute-done.3 = bf16[128,768]{1,0:T(8,128)(2,1)S(1)} collective-permute-done((bf16[128,768]{1,0:T(8,128)(2,1)S(1)}, bf16[128,768]{1,0:T(8,128)(2,1)S(1)}, u32[]{:S(2)}, u32[]{:S(2)}) %collective-permute-start.3) | collective-permute-done | bytes 196640 | tf_op jit(solution)/shard_map/cond/branch_1_fun/ppermute | solution.py:700
  230.6 0.9 maximum_bitcast_fusion
  231.5 6.6 %all-to-all-done.4 = bf16[4,16,88,128]{3,2,1,0:T(8,128)(2,1)S(1)} async-done(((bf16[4,16,88,128]{3,2,1,0:T(8,128)(2,1)}), bf16[4,16,88,128]{3,2,1,0:T(8,128)(2,1)S(1)}, u32[]{:S(2)}, u32[]{:S(2)}) %all-to-all-start.4) | async-done | bytes 1441824 | tf_op jit(solution)/shard_map/cond/branch_1_fun/all_to_all | solution.py:709
  238.3 1.6 unpack.1
  240.5 0.6 select_bitcast_fusion
  241.1 0.6 slice_bitcast_fusion
  241.7 0.6 slice_bitcast_fusion.1
  242.3 5.5 %widen.1 = (f32[1536,768]{1,0:T(8,128)}, f32[768,1536]{1,0:T(8,128)}) custom-call(bf16[1536,768]{1,0:T(8,128)(2,1)} %get-tuple-element.185.contract_ref, bf16[768,1536]{1,0:T(8,128)(2,1)} %get-tuple-element.186.expand_ref), custom_call_target="tpu_custom_call" | custom-call | tf_op jit(solution)/shard_map/widen/pallas_call | solution.py:622
  (113 shorter events, 4.7 us)
Async XLA Ops:
  7.2 10.0 %copy-start = (bf16[1,256,768]{2,1,0:T(8,128)(2,1)S(1)}, bf16[1,256,768]{2,1,0:T(8,128)(2,1)}, u32[]{:S(2)}) copy-start(bf16[1,256,768]{2,1,0:T(8,128)(2,1)} %param.19) | copy-start | bytes 1179652
  7.2 10.0 %copy-start.15 = (bf16[768,128]{1,0:T(8,128)(2,1)S(1)}, bf16[768,128]{1,0:T(8,128)(2,1)}, u32[]{:S(2)}) copy-start(bf16[768,128]{1,0:T(8,128)(2,1)} %weight_ref.1) | copy-start | bytes 589828
  9.3 13.8 %copy-start.22 = (f32[384]{0:T(512)S(1)}, f32[384]{0:T(512)}, u32[]{:S(2)}) copy-start(f32[384]{0:T(512)} %param.23) | copy-start | bytes 4612
  9.3 15.3 %collective-permute-start.10 = (bf16[256,768]{1,0:T(8,128)(2,1)S(1)}, bf16[256,768]{1,0:T(8,128)(2,1)S(1)}, u32[]{:S(2)}, u32[]{:S(2)}) collective-permute-start(bf16[256,768]{1,0:T(8,128)(2,1)S(1)} %pad_maximum_fusion.2), channel_id=1, source_target_pairs={{0,31},{1,30},{2,29},{3,28},{4,27},{5,26},{6,25},{7,24},{8,23},{9,... | collective-permute-start | bytes 1179656 | tf_op jit(solution)/shard_map/ppermute | solution.py:700
  15.1 9.5 %collective-permute-start.11 = (bf16[768,384]{1,0:T(8,128)(2,1)}, bf16[768,384]{1,0:T(8,128)(2,1)}, u32[]{:S(2)}, u32[]{:S(2)}) collective-permute-start(bf16[768,384]{1,0:T(8,128)(2,1)} %mine_ref.3), channel_id=1, source_target_pairs={{0,1},{1,0},{2,3},{3,2},{4,5},{5,4},{6,7},{7,6},{8,9},{9,8},{10,11... | collective-permute-start | bytes 1769480 | tf_op jit(solution)/shard_map/ppermute | solution.py:695
  15.8 7.3 %collective-permute-start.12 = (f32[384]{0:T(512)}, f32[384]{0:T(512)S(1)}, u32[]{:S(2)}, u32[]{:S(2)}) collective-permute-start(f32[384]{0:T(512)} %param.23), channel_id=1, source_target_pairs={{0,1},{1,0},{2,3},{3,2},{4,5},{5,4},{6,7},{7,6},{8,9},{9,8},{10,11... | collective-permute-start | bytes 4616 | tf_op jit(solution)/shard_map/ppermute | solution.py:695
  17.2 0.7 copy-start.3
  19.4 23.7 %all-to-all-start.5 = ((bf16[16,256,128]{2,1,0:T(8,128)(2,1)}), bf16[16,256,128]{2,1,0:T(8,128)(2,1)S(1)}, u32[]{:S(2)}, u32[]{:S(2)}) async-start(bf16[16,256,128]{2,1,0:T(8,128)(2,1)} %own_keyval.1), calls=%async_computation.5 | async-start | bytes 2097152 | tf_op jit(solution)/shard_map/all_to_all | solution.py:709
  23.0 219.3 %all-reduce.3.cloned.1.call-start = ((), (), s32[]{:S(2)}) async-start(), calls=%async_computation.6 | async-start | bytes 9437184 | tf_op jit(solution)/shard_map/psum | solution.py:769
  24.7 18.3 %copy-start.6 = (bf16[384,768]{1,0:T(8,128)(2,1)S(1)}, bf16[384,768]{1,0:T(8,128)(2,1)}, u32[]{:S(2)}) copy-start(bf16[384,768]{1,0:T(8,128)(2,1)} %mine_ref.5) | copy-start | bytes 1769476
  24.7 18.8 %copy-start.19 = (f32[768]{0:T(1024)S(1)}, f32[768]{0:T(1024)}, u32[]{:S(2)}) copy-start(f32[768]{0:T(1024)} %param.28) | copy-start | bytes 9220
  24.7 18.8 %copy-start.20 = (f32[768]{0:T(1024)S(1)}, f32[768]{0:T(1024)}, u32[]{:S(2)}) copy-start(f32[768]{0:T(1024)} %param.27) | copy-start | bytes 9220
  24.7 18.8 %copy-start.21 = (f32[768]{0:T(1024)S(1)}, f32[768]{0:T(1024)}, u32[]{:S(2)}) copy-start(f32[768]{0:T(1024)} %param.29) | copy-start | bytes 9220
  24.7 18.8 %copy-start.25 = (s32[1,8]{1,0:T(1,128)S(1)}, s32[1,8]{1,0:T(1,128)}, u32[]{:S(2)}) copy-start(s32[1,8]{1,0:T(1,128)} %param.35) | copy-start | bytes 100
  27.2 38.7 %copy-start.32 = (bf16[256,768]{1,0:T(8,128)(2,1)}, bf16[256,768]{1,0:T(8,128)(2,1)S(1)}, u32[]{:S(2)}) copy-start(bf16[256,768]{1,0:T(8,128)(2,1)S(1)} %get-tuple-element.147.query_ref) | copy-start | bytes 1179652
  43.0 22.8 %copy-start.11 = (bf16[16,256,128]{2,1,0:T(8,128)(2,1)}, bf16[16,256,128]{2,1,0:T(8,128)(2,1)S(1)}, u32[]{:S(2)}) copy-start(bf16[16,256,128]{2,1,0:T(8,128)(2,1)S(1)} %all-to-all-done.5.own_ref) | copy-start | bytes 3145732
  43.0 3.4 %collective-permute-start.13 = (bf16[16,256,128]{2,1,0:T(8,128)(2,1)S(1)}, bf16[16,256,128]{2,1,0:T(8,128)(2,1)}, u32[]{:S(2)}, u32[]{:S(2)}) collective-permute-start(bf16[16,256,128]{2,1,0:T(8,128)(2,1)S(1)} %all-to-all-done.5.own_ref), channel_id=1, source_target_pairs={{0,1},{1,0},{2,3},{3,2},{4,5},{5,4},{6,7},{7,6},{8,9},{9,8},{10,11... | collective-permute-start | bytes 3145736 | tf_op jit(solution)/shard_map/ppermute | solution.py:695
  43.0 22.9 %collective-permute-start.14 = (bf16[384,768]{1,0:T(8,128)(2,1)S(1)}, bf16[384,768]{1,0:T(8,128)(2,1)S(1)}, u32[]{:S(2)}, u32[]{:S(2)}) collective-permute-start(bf16[384,768]{1,0:T(8,128)(2,1)S(1)} %copy-done.6), channel_id=1, source_target_pairs={{0,1},{1,0},{2,3},{3,2},{4,5},{5,4},{6,7},{7,6},{8,9},{9,8},{10,11... | collective-permute-start | bytes 1769480 | tf_op jit(solution)/shard_map/ppermute | solution.py:695
  44.0 21.8 %copy-start.23 = (s32[2,128]{1,0:T(2,128)}, s32[2,128]{1,0:T(2,128)S(1)}, u32[]{:S(2)}) copy-start(s32[2,128]{1,0:T(2,128)S(1)} %select_reduce_fusion) | copy-start | bytes 3076
  44.0 23.3 %collective-permute-start.16 = (bf16[256,768]{1,0:T(8,128)(2,1)S(1)}, bf16[256,768]{1,0:T(8,128)(2,1)S(1)}, u32[]{:S(2)}, u32[]{:S(2)}) collective-permute-start(bf16[256,768]{1,0:T(8,128)(2,1)S(1)} %pad_maximum_fusion.3.own_grad_ref.grad_ref), channel_id=1, source_target_pairs={{0,1},{1,0},{2,3},{3,2},{4,5},{5,4},{6,7},{7,6},{8,9},{9,8},{10,11... | collective-permute-start | bytes 1179656 | tf_op jit(solution)/shard_map/ppermute | solution.py:695
  46.4 19.5 %copy-start.27 = (bf16[256,768]{1,0:T(8,128)(2,1)S(1)}, bf16[256,768]{1,0:T(8,128)(2,1)}, u32[]{:S(2)}) copy-start(bf16[256,768]{1,0:T(8,128)(2,1)} %get-tuple-element.150.tokens_ref) | copy-start | bytes 1179652
  46.4 22.3 %copy-start.5 = (bf16[1536,768]{1,0:T(8,128)(2,1)S(1)}, bf16[1536,768]{1,0:T(8,128)(2,1)}, u32[]{:S(2)}) copy-start(bf16[1536,768]{1,0:T(8,128)(2,1)} %contract_ref.1) | copy-start | bytes 7077892
  65.9 1.5 copy-start.30
  65.9 1.5 copy-start.17
  65.9 2.8 %copy-start.4 = (bf16[768,1536]{1,0:T(8,128)(2,1)S(1)}, bf16[768,1536]{1,0:T(8,128)(2,1)}, u32[]{:S(2)}) copy-start(bf16[768,1536]{1,0:T(8,128)(2,1)} %expand_ref.1) | copy-start | bytes 7077892
  66.7 2.0 collective-permute-start.15
  77.0 0.7 copy-start.26
  77.0 3.7 %copy-start.12 = (bf16[16,256,128]{2,1,0:T(8,128)(2,1)S(1)}, bf16[16,256,128]{2,1,0:T(8,128)(2,1)}, u32[]{:S(2)}) copy-start(bf16[16,256,128]{2,1,0:T(8,128)(2,1)} %copy-done.11) | copy-start | bytes 3145732
  77.0 3.7 %copy-start.16 = (f32[768]{0:T(1024)S(1)}, f32[768]{0:T(1024)}, u32[]{:S(2)}) copy-start(f32[768]{0:T(1024)} %param.20) | copy-start | bytes 9220
  77.0 3.7 %copy-start.24 = (s32[2,128]{1,0:T(2,128)S(1)}, s32[2,128]{1,0:T(2,128)}, u32[]{:S(2)}) copy-start(s32[2,128]{1,0:T(2,128)} %copy-done.23) | copy-start | bytes 3076
  77.0 3.7 %copy-start.31 = (f32[2,64,1536]{2,1,0:T(8,128)S(1)}, f32[2,64,1536]{2,1,0:T(8,128)}, u32[]{:S(2)}) copy-start(f32[2,64,1536]{2,1,0:T(8,128)} %get-tuple-element.158) | copy-start | bytes 2359300
  77.1 3.7 %copy-start.33 = (bf16[256,768]{1,0:T(8,128)(2,1)S(1)}, bf16[256,768]{1,0:T(8,128)(2,1)}, u32[]{:S(2)}) copy-start(bf16[256,768]{1,0:T(8,128)(2,1)} %copy-done.32) | copy-start | bytes 1179652
  77.1 3.7 %copy-start.34 = (f32[2,1,1536]{2,1,0:T(1,128)S(1)}, f32[2,1,1536]{2,1,0:T(1,128)}, u32[]{:S(2)}) copy-start(f32[2,1,1536]{2,1,0:T(1,128)} %get-tuple-element.159) | copy-start | bytes 36868
  77.1 1.8 collective-permute-start.17
  80.8 37.6 %copy-start.13 = (f32[256,768]{1,0:T(8,128)}, f32[256,768]{1,0:T(8,128)S(1)}, u32[]{:S(2)}) copy-start(f32[256,768]{1,0:T(8,128)S(1)} %get-tuple-element.46) | copy-start | bytes 2359300 | tf_op jit(solution)/shard_map/cond
  118.4 0.7 copy-start.9
  119.1 2.8 %collective-permute-start.2 = (bf16[16,256,128]{2,1,0:T(8,128)(2,1)S(1)}, bf16[16,256,128]{2,1,0:T(8,128)(2,1)S(1)}, u32[]{:S(2)}, u32[]{:S(2)}) collective-permute-start(bf16[16,256,128]{2,1,0:T(8,128)(2,1)S(1)} %get-tuple-element.59), channel_id=1, source_target_pairs={{0,1},{1,0},{2,3},{3,2},{4,5},{5,4},{6,7},{7,6},{8,9},{9,8},{10,11... | collective-permute-start | bytes 3145736 | tf_op jit(solution)/shard_map/cond/branch_1_fun/ppermute | solution.py:695
  123.1 23.4 %all-to-all-start = ((bf16[16,256,128]{2,1,0:T(8,128)(2,1)}), bf16[16,256,128]{2,1,0:T(8,128)(2,1)S(1)}, u32[]{:S(2)}, u32[]{:S(2)}) async-start(bf16[16,256,128]{2,1,0:T(8,128)(2,1)} %add_convert_fusion), calls=%async_computation | async-start | bytes 2097152 | tf_op jit(solution)/shard_map/cond/branch_1_fun/all_to_all | solution.py:709
  126.8 1.0 copy-start.10
  131.3 0.9 copy-start.7
  132.2 14.3 %copy-start.28 = (f32[8,768]{1,0:T(8,128)S(1)}, f32[8,768]{1,0:T(8,128)}, u32[]{:S(2)}) copy-start(f32[8,768]{1,0:T(8,128)} %get-tuple-element.71.middle_sums_ref) | copy-start | bytes 73732 | tf_op jit(solution)/shard_map/cond
  132.2 14.3 %copy-start.29 = (f32[1,1536]{1,0:T(1,128)S(1)}, f32[1,1536]{1,0:T(1,128)}, u32[]{:S(2)}) copy-start(f32[1,1536]{1,0:T(1,128)} %get-tuple-element.73.expand_bias_ref) | copy-start | bytes 18436 | tf_op jit(solution)/shard_map/cond
  132.2 2.3 collective-permute-start.4
  132.6 2.8 %collective-permute-start.5 = (bf16[384,768]{1,0:T(8,128)(2,1)}, bf16[384,768]{1,0:T(8,128)(2,1)}, u32[]{:S(2)}, u32[]{:S(2)}) collective-permute-start(bf16[384,768]{1,0:T(8,128)(2,1)} %get-tuple-element.79), channel_id=1, source_target_pairs={{0,1},{1,0},{2,3},{3,2},{4,5},{5,4},{6,7},{7,6},{8,9},{9,8},{10,11... | collective-permute-start | bytes 1769480 | tf_op jit(solution)/shard_map/cond/branch_1_fun/ppermute | solution.py:695
  137.8 0.8 copy-start.1
  138.6 11.9 %collective-permute-start.6 = (bf16[1152,128]{1,0:T(8,128)(2,1)}, bf16[1152,128]{1,0:T(8,128)(2,1)S(1)}, u32[]{:S(2)}, u32[]{:S(2)}) collective-permute-start(bf16[1152,128]{1,0:T(8,128)(2,1)} %get-tuple-element.82), channel_id=1, source_target_pairs={{0,32},{32,64},{64,96},{96,0},{1,33},{33,65},{65,97},{97,1},{2,34}... | collective-permute-start | bytes 884744 | tf_op jit(solution)/shard_map/cond/branch_1_fun/ppermute | solution.py:792
  140.2 17.0 %collective-permute-start.7 = (bf16[1152,128]{1,0:T(8,128)(2,1)}, bf16[1152,128]{1,0:T(8,128)(2,1)}, u32[]{:S(2)}, u32[]{:S(2)}) collective-permute-start(bf16[1152,128]{1,0:T(8,128)(2,1)} %get-tuple-element.83), channel_id=1, source_target_pairs={{0,64},{32,96},{64,0},{96,32},{1,65},{33,97},{65,1},{97,33},{2,66}... | collective-permute-start | bytes 884744 | tf_op jit(solution)/shard_map/cond/branch_1_fun/ppermute | solution.py:792
  143.1 14.1 %collective-permute-start.8 = (bf16[1152,128]{1,0:T(8,128)(2,1)}, bf16[1152,128]{1,0:T(8,128)(2,1)}, u32[]{:S(2)}, u32[]{:S(2)}) collective-permute-start(bf16[1152,128]{1,0:T(8,128)(2,1)} %get-tuple-element.84), channel_id=1, source_target_pairs={{0,96},{32,0},{64,32},{96,64},{1,97},{33,1},{65,33},{97,65},{2,98}... | collective-permute-start | bytes 884744 | tf_op jit(solution)/shard_map/cond/branch_1_fun/ppermute | solution.py:792
  146.5 1.1 copy-start.8
  147.6 13.4 %copy-start.2 = (f32[1152,128]{1,0:T(8,128)S(1)}, f32[1152,128]{1,0:T(8,128)}, u32[]{:S(2)}) copy-start(f32[1152,128]{1,0:T(8,128)} %copy-done.1) | copy-start | bytes 1769476 | tf_op jit(solution)/shard_map/cond
  157.3 10.5 %all-to-all-start.1 = ((bf16[4,256,128]{2,1,0:T(8,128)(2,1)}), bf16[4,256,128]{2,1,0:T(8,128)(2,1)S(1)}, u32[]{:S(2)}, u32[]{:S(2)}) async-start(bf16[4,256,128]{2,1,0:T(8,128)(2,1)} %bitcast.4), calls=%async_computation.1 | async-start | bytes 524288 | tf_op jit(solution)/shard_map/cond/branch_1_fun/all_to_all | solution.py:709
  168.5 16.2 %all-to-all-start.2 = ((bf16[16,88,128]{2,1,0:T(8,128)(2,1)}), bf16[16,88,128]{2,1,0:T(8,128)(2,1)S(1)}, u32[]{:S(2)}, u32[]{:S(2)}) async-start(bf16[16,88,128]{2,1,0:T(8,128)(2,1)} %pad_maximum_fusion), calls=%async_computation.2 | async-start | bytes 720896 | tf_op jit(solution)/shard_map/cond/branch_1_fun/all_to_all | solution.py:709
  184.8 1.3 collective-permute-start.9
  186.9 14.5 %all-to-all-start.3 = ((bf16[16,88,128]{2,1,0:T(8,128)(2,1)}), bf16[16,88,128]{2,1,0:T(8,128)(2,1)S(1)}, u32[]{:S(2)}, u32[]{:S(2)}) async-start(bf16[16,88,128]{2,1,0:T(8,128)(2,1)} %broadcast_in_dim.34), calls=%async_computation.3 | async-start | bytes 720896 | tf_op jit(solution)/shard_map/cond/branch_1_fun/all_to_all | solution.py:709
  190.5 15.9 %copy-start.14 = (f32[256,768]{1,0:T(8,128)S(1)}, f32[256,768]{1,0:T(8,128)}, u32[]{:S(2)}) copy-start(f32[256,768]{1,0:T(8,128)} %copy-done.13) | copy-start | bytes 2359300 | tf_op jit(solution)/shard_map/cond
  190.5 15.9 %copy-start.18 = (f32[768]{0:T(1024)S(1)}, f32[768]{0:T(1024)}, u32[]{:S(2)}) copy-start(f32[768]{0:T(1024)} %get-tuple-element.184) | copy-start | bytes 9220 | tf_op jit(solution)/shard_map/cond
  190.5 15.8 %collective-permute-start = (bf16[256,768]{1,0:T(8,128)(2,1)}, bf16[256,768]{1,0:T(8,128)(2,1)}, u32[]{:S(2)}, u32[]{:S(2)}) collective-permute-start(bf16[256,768]{1,0:T(8,128)(2,1)} %get-tuple-element.48), channel_id=1, source_target_pairs={{0,1},{1,0},{2,3},{3,2},{4,5},{5,4},{6,7},{7,6},{8,9},{9,8},{10,11... | collective-permute-start | bytes 1179656 | tf_op jit(solution)/shard_map/cond/branch_1_fun/ppermute | solution.py:695
  202.8 35.4 %all-to-all-start.4 = ((bf16[4,16,88,128]{3,2,1,0:T(8,128)(2,1)}), bf16[4,16,88,128]{3,2,1,0:T(8,128)(2,1)S(1)}, u32[]{:S(2)}, u32[]{:S(2)}) async-start(bf16[4,16,88,128]{3,2,1,0:T(8,128)(2,1)} %broadcast_in_dim.35), calls=%async_computation.4 | async-start | bytes 2883584 | tf_op jit(solution)/shard_map/cond/branch_1_fun/all_to_all | solution.py:709
  207.9 14.4 %collective-permute-start.1 = (bf16[128,768]{1,0:T(8,128)(2,1)S(1)}, bf16[128,768]{1,0:T(8,128)(2,1)S(1)}, u32[]{:S(2)}, u32[]{:S(2)}) collective-permute-start(bf16[128,768]{1,0:T(8,128)(2,1)S(1)} %get-tuple-element.188), channel_id=1, source_target_pairs={{0,31},{1,30},{2,29},{3,28},{4,27},{5,26},{6,25},{7,24},{8,23},{9,... | collective-permute-start | bytes 589832 | tf_op jit(solution)/shard_map/cond/branch_1_fun/ppermute | solution.py:700
  208.3 22.2 %collective-permute-start.3 = (bf16[128,768]{1,0:T(8,128)(2,1)S(1)}, bf16[128,768]{1,0:T(8,128)(2,1)S(1)}, u32[]{:S(2)}, u32[]{:S(2)}) collective-permute-start(bf16[128,768]{1,0:T(8,128)(2,1)S(1)} %get-tuple-element.75), channel_id=1, source_target_pairs={{0,31},{1,30},{2,29},{3,28},{4,27},{5,26},{6,25},{7,24},{8,23},{9,... | collective-permute-start | bytes 589832 | tf_op jit(solution)/shard_map/cond/branch_1_fun/ppermute | solution.py:700
Sparse Core Ops, SparseCore 0:
  77.1 159.6 all-reduce.2
where the time goes:
time: 256 us; the launch traced here: 255 us
  Pallas kernels  87.9 us (34%)
  waiting for transfers between devices  85.7 us (33%)
  starting transfers between devices  45.7 us (18%)
  between operations  14.4 us (6%)
  local copies, waits for them, and re-layouts  13 us (5%)
  other arithmetic  7.68 us (3%)
    all_to_all x6, waiting for transfers between devices, spread_out(): return lax.all_to_all(blocks, axis, split_axis=0, concat_axis=0, tiled=True)  49.9 us
    pallas_call x1, Pallas kernels, attend_back(): pl.pallas_call(backward_kernel, out_shape=(jax.ShapeDtypeStruct((rows, wi...  37.5 us
    all_to_all x6, starting transfers between devices, spread_out(): return lax.all_to_all(blocks, axis, split_axis=0, concat_axis=0, tiled=True)  25.1 us
    pallas_call x8, Pallas kernels, run(): pl.pallas_call(kernel, out_shape=outs, in_specs=[VM] * len(args), out_spe...  23 us
    pallas_call x1, Pallas kernels, attend(): pl.pallas_call(forward_kernel, out_shape=(jax.ShapeDtypeStruct((rows, wid...  19.4 us
    ppermute x3, waiting for transfers between devices, opposite(): lax.ppermute(value, ('seq', 'heads'), [(i, count - 1 - i) for i in range(...  18.3 us
    ppermute x3, starting transfers between devices, opposite(): lax.ppermute(value, ('seq', 'heads'), [(i, count - 1 - i) for i in range(...  11 us
    ppermute x12, waiting for transfers between devices, swapped(): return lax.ppermute(value, 'heads', SWAP)  10.9 us
  transfers between devices with their start and end apart: 25, of which 17 were waited for; matrix products, arithmetic and copies ran while one was open for 5% of the time, Pallas kernels for 29%

commit v1 on v0

--- a/solution.py
+++ b/solution.py
@@ -340,6 +340,10 @@
     return lax.dot_general(left, right, (((1,), (1,)), ((), ())), preferred_element_type=jnp.float32)
 
 
+def line(ref):
+    return ref[...].reshape(1, ref.shape[0])
+
+
 def statistics(values):
     center = values - jnp.mean(values, axis=-1, keepdims=True)
     spread = jnp.mean(center * center, axis=-1, keepdims=True)
@@ -352,33 +356,36 @@
 ):
     width = mine_ref.shape[0]
     rows = mm(attended_ref[:, :width], mine_ref[...]) + mm(attended_ref[:, width:], theirs_ref[...])
-    middle = tokens_ref[...].astype(jnp.float32) + rows + bias_ref[...]
+    middle = tokens_ref[...].astype(jnp.float32) + rows + line(bias_ref)
     middle_ref[...] = middle
     normal, _ = statistics(middle)
-    normed_ref[...] = (normal * gain_ref[...] + shift_ref[...]).astype(jnp.bfloat16)
-
-
-def own_kernel(tokens_ref, gain_ref, shift_ref, weight_ref, bias_ref, blocks_ref):
+    normed_ref[...] = (normal * line(gain_ref) + line(shift_ref)).astype(jnp.bfloat16)
+
+
+def own_kernel(tokens_ref, cotangent_ref, gain_ref, shift_ref, weight_ref, bias_ref, blocks_ref, halves_ref):
+    half = tokens_ref.shape[0] // 2
+    halves_ref[:half, :] = tokens_ref[half:, :]
+    halves_ref[half:, :] = cotangent_ref[half:, :]
     normal, _ = statistics(tokens_ref[...].astype(jnp.float32))
-    normed = (normal * gain_ref[...] + shift_ref[...]).astype(jnp.bfloat16)
-    bias = jnp.concatenate([jnp.zeros_like(bias_ref[...]), bias_ref[...]], axis=1)
+    normed = (normal * line(gain_ref) + line(shift_ref)).astype(jnp.bfloat16)
+    bias = jnp.concatenate([jnp.zeros_like(line(bias_ref)), line(bias_ref)], axis=1)
     keyval = (mm(normed, weight_ref[...]) + bias).astype(jnp.bfloat16)
     for i in range(blocks_ref.shape[0]):
         blocks_ref[i] = keyval
 
 
 def query_kernel(
-    own_ref, half_ref, gain_ref, shift_ref, mine_ref, theirs_ref, mine_bias_ref, theirs_bias_ref,
+    own_ref, received_ref, gain_ref, shift_ref, mine_ref, theirs_ref, mine_bias_ref, theirs_bias_ref,
     tokens_ref, normed_ref, query_ref,
 ):
-    half, width = half_ref.shape[0], mine_ref.shape[1]
+    half, width = received_ref.shape[0] // 2, mine_ref.shape[1]
     tokens_ref[:half, :] = own_ref[:half, :]
-    tokens_ref[half:, :] = half_ref[...]
+    tokens_ref[half:, :] = received_ref[:half, :]
     normal, _ = statistics(tokens_ref[...].astype(jnp.float32))
-    normed = (normal * gain_ref[...] + shift_ref[...]).astype(jnp.bfloat16)
+    normed = (normal * line(gain_ref) + line(shift_ref)).astype(jnp.bfloat16)
     normed_ref[...] = normed
-    mine = (mm(normed, mine_ref[...]) + mine_bias_ref[...]).astype(jnp.bfloat16)
-    theirs = (mm(normed, theirs_ref[...]) + theirs_bias_ref[...]).astype(jnp.bfloat16)
+    mine = (mm(normed, mine_ref[...]) + line(mine_bias_ref)).astype(jnp.bfloat16)
+    theirs = (mm(normed, theirs_ref[...]) + line(theirs_bias_ref)).astype(jnp.bfloat16)
     query_ref[:, :width] = mine * jnp.bfloat16(0.125)
     query_ref[:, width:] = theirs * jnp.bfloat16(0.125)
 
@@ -400,8 +407,10 @@
     def products(cols):
         return mm(both[...], expand_ref[:, cols]), mm_cols(grads[...], contract_ref[cols, :])
 
+    bias = line(bias_ref)
+
     def activate(cols, inner, acts_grad):
-        inner = inner + bias_ref[:, cols]
+        inner = inner + bias[:, cols]
         square = inner * inner
         tanh = jnp.tanh(inner * (ROOT + ROOT * CUBE * square))
         half = 0.5 + 0.5 * tanh
@@ -444,7 +453,7 @@
     back = back_ref[...] + peer_back_ref[...].astype(jnp.float32)
     grad = grad_ref[...].astype(jnp.float32)
     normal, scale = statistics(middle_ref[...])
-    weighted = back * gain_ref[...]
+    weighted = back * line(gain_ref)
     mean = jnp.mean(weighted, axis=-1, keepdims=True)
     along = jnp.mean(weighted * normal, axis=-1, keepdims=True)
     middle_grad = grad + scale * (weighted - mean - normal * along)
@@ -461,17 +470,23 @@
 
 def query_back_kernel(
     grad_ref, normed_ref, attended_ref, low_ref, mine_ref, theirs_ref,
-    normed_grad_ref, mine_part_ref, theirs_part_ref, mine_out_ref, theirs_out_ref, bias_ref,
+    normed_grad_ref, mine_part_ref, theirs_part_ref, bias_ref,
 ):
     width = mine_ref.shape[1]
     normed = normed_ref[...].T
     attended = attended_ref[...].T
     mine, theirs = grad_ref[:, :width], grad_ref[:, width:]
     normed_grad_ref[...] = mm_cols(mine, mine_ref[...]) + mm_cols(theirs, theirs_ref[...])
-    theirs_part_ref[...] = mm(normed, theirs).astype(jnp.bfloat16)
-    theirs_out_ref[...] = mm(attended[width:], low_ref[...]).astype(jnp.bfloat16)
-    mine_part_ref[...] = mm(normed, mine)
-    mine_out_ref[...] = mm(attended[:width], low_ref[...])
+
+    def put(ref, *parts):
+        place = 0
+        for part in parts:
+            for col in range(0, part.shape[1], HALF):
+                ref[place : place + part.shape[0], :] = part[:, col : col + HALF].astype(ref.dtype)
+                place += part.shape[0]
+
+    put(theirs_part_ref, mm(normed, theirs), mm(attended[width:], low_ref[...]))
+    put(mine_part_ref, mm(normed, mine), mm(attended[:width], low_ref[...]))
     bias_ref[...] = jnp.sum(grad_ref[...].astype(jnp.float32), axis=0, keepdims=True)
 
 
@@ -486,7 +501,7 @@
     grad = grad.astype(jnp.bfloat16)
     back = normed_grad_ref[...] + mm_cols(grad, weight_ref[...])
     normal, scale = statistics(tokens_ref[...].astype(jnp.float32))
-    weighted = back * gain_ref[...]
+    weighted = back * line(gain_ref)
     mean = jnp.mean(weighted, axis=-1, keepdims=True)
     along = jnp.mean(weighted * normal, axis=-1, keepdims=True)
     tokens_grad = middle_grad_ref[...] + scale * (weighted - mean - normal * along)
@@ -519,36 +534,38 @@
     sent_ref[place:, :] = jnp.zeros_like(sent_ref[place:, :])
 
 
-def pack_kernel(
-    win_ref, query_ref, peer_query_ref, out_ref, peer_out_ref, own_ref, first_ref, second_ref, third_ref, packed
-):
-    place = 0
-    for ref, peer in ((query_ref, peer_query_ref), (out_ref, peer_out_ref)):
-        depth = ref.shape[0]
-        for col in range(0, ref.shape[1], HALF):
-            span = slice(col, col + HALF)
-            packed[place : place + depth, :] = ref[:, span] + peer[:, span].astype(jnp.float32)
-            place += depth
+def pack_kernel(win_ref, part_ref, peer_ref, own_ref, first_ref, second_ref, third_ref):
     depth = own_ref.shape[0]
-    count = place // depth
+    count = part_ref.shape[0] // depth
     for shift, ref in enumerate((own_ref, first_ref, second_ref, third_ref)):
         to = lax.rem(win_ref[0] + shift, count)
         rows = pl.ds(pl.multiple_of(to * depth, HALF), depth)
-        ref[...] = packed[rows, :].astype(ref.dtype)
-
-
-def unpack_kernel(weights_ref, rest_ref, query_ref, out_ref, keyval_ref, rows_ref):
+        ref[...] = (part_ref[rows, :] + peer_ref[rows, :].astype(jnp.float32)).astype(ref.dtype)
+
+
+def unpack_kernel(
+    win_ref, own_ref, first_ref, second_ref, third_ref, query_ref, out_ref, keyval_ref, rows_ref, weights_ref, rest_ref
+):
+    pieces_of = (own_ref, first_ref, second_ref, third_ref)
+    count = own_ref.shape[0]
+    depth = weights_ref.shape[0] // len(pieces_of) // count
+    spare = rest_ref.shape[0] // len(pieces_of) // count
+    for shift, ref in enumerate(pieces_of):
+        start = lax.rem(win_ref[0] + len(pieces_of) - shift, len(pieces_of)) * count
+        for i in range(count):
+            piece = ref[i].astype(jnp.float32)
+            weights_ref[pl.ds(pl.multiple_of((start + i) * depth, 8), depth), :] = piece[:depth]
+            rest_ref[pl.ds(pl.multiple_of((start + i) * spare, 8), spare), :] = piece[depth:]
     place = 0
     for ref in (query_ref, out_ref):
         depth = ref.shape[0]
         for col in range(0, ref.shape[1], HALF):
-            ref[:, col : col + HALF] = weights_ref[place : place + depth, :].astype(jnp.float32)
+            ref[:, col : col + HALF] = weights_ref[place : place + depth, :]
             place += depth
     place = keyval_ref.shape[0]
-    keyval_ref[...] = rest_ref[:place, :].astype(jnp.float32)
+    keyval_ref[...] = rest_ref[:place, :]
     depth = rows_ref.shape[0]
-    high = rest_ref[place : place + depth, :].astype(jnp.float32)
-    rows_ref[...] = high + rest_ref[place + depth : place + 2 * depth, :].astype(jnp.float32)
+    rows_ref[...] = rest_ref[place : place + depth, :] + rest_ref[place + depth : place + 2 * depth, :]
 
 
 def like(*shape, dtype=jnp.float32):
@@ -570,21 +587,22 @@
 
 def residual(attended, tokens, pair, bias, gain, shift):
     outs = (like(*tokens.shape), like(*tokens.shape, dtype=jnp.bfloat16))
-    rows = (bias[None], gain[None], shift[None])
-    return run(residual_kernel, outs, [], 12, 10**9, "residual", attended, tokens, *pair, *rows)
-
-
-def own_keyval_blocks(tokens, gain, shift, weight, bias, count):
-    outs = (like(count, tokens.shape[0], weight.shape[1], dtype=jnp.bfloat16),)
-    return run(own_kernel, outs, [], 8, 10**8, "own_keyval", tokens, gain[None], shift[None], weight, bias[None])[0]
-
-
-def query_rows(own, half, gain, shift, pair, biases):
+    return run(residual_kernel, outs, [], 12, 10**9, "residual", attended, tokens, *pair, bias, gain, shift)
+
+
+def own_keyval_blocks(tokens, cotangent, gain, shift, weight, bias, count):
+    outs = (
+        like(count, tokens.shape[0], weight.shape[1], dtype=jnp.bfloat16),
+        like(*tokens.shape, dtype=jnp.bfloat16),
+    )
+    return run(own_kernel, outs, [], 60, 10**8, "own_keyval", tokens, cotangent, gain, shift, weight, bias)
+
+
+def query_rows(own, received, gain, shift, pair, biases):
     low16 = like(*own.shape, dtype=jnp.bfloat16)
-    rows = (gain[None], shift[None])
     outs = (low16, low16, low16)
     return run(
-        query_kernel, outs, [], 12, 3 * 10**10, "query_rows", own, half, *rows, *pair, biases[0][None], biases[1][None]
+        query_kernel, outs, [], 12, 3 * 10**10, "query_rows", own, received, gain, shift, *pair, *biases
     )
 
 
@@ -609,7 +627,7 @@
         pltpu.VMEM((2 * rows, hidden), b16),
     ]
     return run(
-        mlp_kernel, outs, scratch, 32, 10**10, "mlp", own, peer, own_grad, peer_grad, expand, bias[None], contract
+        mlp_kernel, outs, scratch, 32, 10**10, "mlp", own, peer, own_grad, peer_grad, expand, bias, contract
     )
 
 
@@ -635,7 +653,7 @@
     b16 = jnp.bfloat16
     outs = (like(rows, features), like(rows, features, dtype=b16), like(rows, features, dtype=b16), like(8, features))
     return run(
-        residual_back_kernel, outs, [], 12, 10**9, "residual_back", back, peer_back, grad, middle, gain[None], *pair
+        residual_back_kernel, outs, [], 12, 10**9, "residual_back", back, peer_back, grad, middle, gain, *pair
     )
 
 
@@ -648,43 +666,53 @@
     b16 = jnp.bfloat16
     outs = (
         like(rows, features),
-        like(features, width),
-        like(features, width, dtype=b16),
-        like(width, features),
-        like(width, features, dtype=b16),
+        like(2 * features * width // HALF, HALF),
+        like(2 * features * width // HALF, HALF, dtype=b16),
         like(1, features),
     )
     return run(query_back_kernel, outs, [], 16, 10**10, "query_back", grad, normed, attended, lowered, *pair)
 
 
 def token_back(ranks, arrived, normed_grad, weight, tokens, gain, normed, middle_grad, vectors):
-    rows, features = normed.shape
+    count, features = normed.shape
     depth = weight.shape[0] + 2 * VECTOR_ROWS
     depth += -depth % (16 * ranks)
-    outs = (like(rows // 2, features), like(rows // 2, features, dtype=jnp.bfloat16), like(depth, HALF, dtype=jnp.bfloat16))
+    outs = (
+        like(count // 2, features),
+        like(count // 2, features, dtype=jnp.bfloat16),
+        like(depth, HALF, dtype=jnp.bfloat16),
+    )
     return run(
         token_back_kernel, outs, [pltpu.VMEM((VECTOR_ROWS, HALF), jnp.float32)], 12, 10**9, "token_back",
-        arrived, normed_grad, weight, tokens, gain[None], normed, middle_grad, *vectors,
-    )
-
-
-def pack(win, query_part, peer_query, out_part, peer_out):
-    depth = (query_part.size + out_part.size) // HALF // 4
+        arrived, normed_grad, weight, tokens, gain, normed, middle_grad, *vectors,
+    )
+
+
+def pack(win, part, peer):
+    depth = part.shape[0] // 4
     outs = (like(depth, HALF), *(like(depth, HALF, dtype=jnp.bfloat16) for _ in range(3)))
     return pl.pallas_call(
         pack_kernel,
         out_shape=outs,
+        in_specs=[SM] + [VM] * 2,
+        out_specs=(VM,) * 4,
+        compiler_params=pltpu.CompilerParams(vmem_limit_bytes=16 * 2**20),
+        name="pack",
+    )(win, part, peer)
+
+
+def unpack(win, parts, rest_rows, query_shape, out_shape, keyval_shape):
+    outs = (like(*query_shape), like(*out_shape), like(*keyval_shape), like(VECTOR_ROWS, HALF))
+    weight_rows = (math.prod(query_shape) + math.prod(out_shape)) // HALF
+    return pl.pallas_call(
+        unpack_kernel,
+        out_shape=outs,
         in_specs=[SM] + [VM] * 4,
         out_specs=(VM,) * 4,
-        scratch_shapes=[pltpu.VMEM((4 * depth, HALF), jnp.float32)],
-        compiler_params=pltpu.CompilerParams(vmem_limit_bytes=16 * 2**20),
-        name="pack",
-    )(win, query_part, peer_query, out_part, peer_out)
-
-
-def unpack(weights, rest, query_shape, out_shape, keyval_shape):
-    outs = (like(*query_shape), like(*out_shape), like(*keyval_shape), like(VECTOR_ROWS, HALF))
-    return run(unpack_kernel, outs, [], 12, 10**8, "unpack", weights, rest)
+        scratch_shapes=[pltpu.VMEM((weight_rows, HALF), jnp.float32), pltpu.VMEM((rest_rows, HALF), jnp.float32)],
+        compiler_params=pltpu.CompilerParams(vmem_limit_bytes=20 * 2**20),
+        name="unpack",
+    )(win, *parts)
 
 
 def low(value):
@@ -737,12 +765,11 @@
     places = place.astype(jnp.int32).reshape(1)
     ranks = lax.axis_size(("win", "seq"))
 
-    received = opposite(jnp.concatenate([tokens[0, HALF:], cotangent[0, HALF:]]))
-    tokens_half = received[:HALF]
+    own_blocks, halves = own_keyval_blocks(
+        tokens[0], cotangent[0], first_gain, first_shift, keyval_weight, value_bias, lax.axis_size("seq")
+    )
+    received = opposite(halves)
     grad_low = jnp.concatenate([cotangent[0, :HALF], received[HALF:]])
-    own_blocks = own_keyval_blocks(
-        tokens[0], first_gain, first_shift, keyval_weight, value_bias, lax.axis_size("seq")
-    )
     own_blocks = spread_out(own_blocks, "seq")
     query_pair = (query_weight, swapped(query_weight))
     out_pair = (out_weight, swapped(out_weight))
@@ -755,7 +782,7 @@
     starts = starts.astype(jnp.int32).reshape(2, 1, HALF)
 
     tokens_low, normed_low, query8 = query_rows(
-        tokens[0], tokens_half, first_gain, first_shift, query_pair, query_biases
+        tokens[0], received, first_gain, first_shift, query_pair, query_biases
     )
     own_blocks, query8 = lax.optimization_barrier((own_blocks, query8))
     peer_blocks = swapped(own_blocks)
@@ -779,7 +806,7 @@
         block_out = exchanged(low(middle + mlp_out + contract_bias))
         pair_grad = low(mine.astype(f32) + swapped(theirs).astype(f32))
         arrived = spread_out(pair_grad, "seq")
-        from_query, query_part, query_sent, out_part, out_sent, query_bias_part = query_back(
+        from_query, weights_part, weights_sent, query_bias_part = query_back(
             query_grad, normed_low, attended, middle_low, query_pair
         )
         core = lax.axis_index("heads")
@@ -787,9 +814,9 @@
         query_bias_part = jnp.where(core == 0, query_bias_part, turned_bias)
         wins, seqs = lax.axis_size("win"), lax.axis_size("seq")
         win = lax.axis_index("win").astype(jnp.int32)
-        kept, *given = pack(win.reshape(1), query_part, swapped(query_sent), out_part, swapped(out_sent))
+        kept, *given = pack(win.reshape(1), weights_part, swapped(weights_sent))
         taken = [
-            lax.ppermute(g, "win", [(i, (i + shift) % wins) for i in range(wins)]) for shift, g in enumerate(given, 1)
+            lax.ppermute(given[shift - 1], "win", [(i, (i + shift) % wins) for i in range(wins)]) for shift in (2, 1, 3)
         ]
         tokens_grad, half, sent = token_back(
             ranks, arrived, from_query, keyval_weight, tokens_low, first_gain, normed_low, middle_grad,
@@ -812,20 +839,24 @@
         shared = shared | ((row >= vectors + VECTOR_ROWS) & (row < vectors + VECTOR_ROWS + common))
         rest = rest + jnp.where(shared, swapped(rest), 0.0)
         full = low(jnp.concatenate([summed[:depth], rest]))
-        full = copies(copies(full, "seq"), "win")
-        query_total, out_total, keyval_total, rows = unpack(
-            full[:, :, :depth].reshape(-1, HALF),
-            full[:, :, depth:].reshape(-1, HALF),
+        full = copies(full, "seq")
+        others = {
+            shift: lax.ppermute(full, "win", [(i, (i + shift) % wins) for i in range(wins)]) for shift in (2, 1, 3)
+        }
+        query_total, out_total, keyval_total, summed_rows = unpack(
+            win.reshape(1),
+            (full, others[1], others[2], others[3]),
+            sent.shape[0],
             query_weight.shape,
             out_weight.shape,
             keyval_weight.shape,
         )
-        rows = rows.reshape(-1)
+        summed_rows = summed_rows.reshape(-1)
         sizes = [features] * 7 + [HALF, expand_bias.shape[0]]
         totals = []
         for size in sizes:
-            totals.append(rows[:size])
-            rows = rows[size:]
+            totals.append(summed_rows[:size])
+            summed_rows = summed_rows[size:]
         query_bias_total = jnp.where(core == 0, totals[6][:width], totals[6][width:])
         return (
             block_out[None],

time: 256 us -> 244 us (0.953)
  local copies, waits for them, and re-layouts: 13 us -> 5.03 us
    psum x1, waiting for transfers between devices: 0.01 us -> 14.6 us  [per_device(): lax.psum((contract_part, expand_part), ('win', 'seq'))]
    all_to_all x6 -> x5, waiting for transfers between devices: 49.9 us -> 37.5 us  [spread_out(): return lax.all_to_all(blocks, axis, split_axis=0, concat_axis=0, tiled=True)]
    ppermute x12 -> x11, waiting for transfers between devices: 10.9 us -> 6.06 us  [swapped(): return lax.ppermute(value, 'heads', SWAP)]
    all_to_all x6 -> x5, starting transfers between devices: 25.1 us -> 21.4 us  [spread_out(): return lax.all_to_all(blocks, axis, split_axis=0, concat_axis=0, tiled=True)]
    ppermute x3 -> x6, starting transfers between devices: 5.83 us -> 9.56 us  [the longest x3 6.44 us: rest(): lax.ppermute(given[shift - 1], 'win', [(i, (i + shift) % wins) for i in r...]
    pallas_call x8 -> x7, Pallas kernels: 23 us -> 24.6 us  [run(): pl.pallas_call(kernel, out_shape=outs, in_specs=[VM] * len(args), out_spe...]
    ppermute x3 -> x6, waiting for transfers between devices: 6.67 us -> 6.71 us  [the longest x3 6.7 us: rest(): lax.ppermute(full, 'win', [(i, (i + shift) % wins) for i in range(wins)])]
  transfers between devices with their start and end apart: 25 -> 26, of which waited for: 17 -> 15; matrix products, arithmetic and copies ran while one was open for 5% -> 3% of each run, Pallas kernels for 29% -> 31%
where the time goes in v1:
time: 244 us; the launch traced here: 243 us
  Pallas kernels  89.9 us (37%)
  waiting for transfers between devices  83.9 us (34%)
  starting transfers between devices  44.5 us (18%)
  between operations  14.3 us (6%)
  other arithmetic  5.22 us (2%)
  local copies, waits for them, and re-layouts  5.03 us (2%)
    pallas_call x1, Pallas kernels, attend_back(): pl.pallas_call(backward_kernel, out_shape=(jax.ShapeDtypeStruct((rows, wi...  37.5 us
    all_to_all x5, waiting for transfers between devices, spread_out(): return lax.all_to_all(blocks, axis, split_axis=0, concat_axis=0, tiled=True)  37.5 us
    pallas_call x7, Pallas kernels, run(): pl.pallas_call(kernel, out_shape=outs, in_specs=[VM] * len(args), out_spe...  24.6 us
    all_to_all x5, starting transfers between devices, spread_out(): return lax.all_to_all(blocks, axis, split_axis=0, concat_axis=0, tiled=True)  21.4 us
    pallas_call x1, Pallas kernels, attend(): pl.pallas_call(forward_kernel, out_shape=(jax.ShapeDtypeStruct((rows, wid...  19.5 us
    ppermute x3, waiting for transfers between devices, opposite(): lax.ppermute(value, ('seq', 'heads'), [(i, count - 1 - i) for i in range(...  19.1 us
    psum x1, waiting for transfers between devices, per_device(): lax.psum((contract_part, expand_part), ('win', 'seq'))  14.6 us
    ppermute x3, starting transfers between devices, opposite(): lax.ppermute(value, ('seq', 'heads'), [(i, count - 1 - i) for i in range(...  11.2 us
  transfers between devices with their start and end apart: 26, of which 15 were waited for; matrix products, arithmetic and copies ran while one was open for 3% of the time, Pallas kernels for 31%

profile of v1, /device:TPU:0, one launch (start us, length us, event | category | flops | bytes accessed | tf_op | source)
XLA Modules:
  0.0 243.3 jit_solution(5663443005972126307)
XLA Ops:
  7.2 0.1 collective-permute-start.13
  7.3 2.8 %own_keyval.1 = (bf16[16,256,128]{2,1,0:T(8,128)(2,1)}, bf16[256,768]{1,0:T(8,128)(2,1)}) custom-call(bf16[256,768]{1,0:T(8,128)(2,1)} %bitcast.38, bf16[256,768]{1,0:T(8,128)(2,1)} %bitcast.41, f32[768]{0:T(1024)} %gain_ref.5, f32[768]{0:T(1024)} %shift_ref.4, bf16[768,128]{1,0:T(8,128)(2,1)} %weight_ref.1, f32[64]{0:T(128)} %bias_ref.3), custom_call_target="tpu_custom_call" | custom-call | flops 100000000 | bytes 1048576 | tf_op jit(solution)/shard_map/own_keyval/pallas_call | solution.py:576
  10.1 6.4 %collective-permute-start.12 = (bf16[256,768]{1,0:T(8,128)(2,1)}, bf16[256,768]{1,0:T(8,128)(2,1)S(1)}, u32[]{:S(2)}, u32[]{:S(2)}) collective-permute-start(bf16[256,768]{1,0:T(8,128)(2,1)} %get-tuple-element.147), channel_id=1, source_target_pairs={{0,31},{1,30},{2,29},{3,28},{4,27},{5,26},{6,25},{7,24},{8,23},{9,... | collective-permute-start | bytes 1179656 | tf_op jit(solution)/shard_map/ppermute | solution.py:728
  16.5 3.7 %all-to-all-start.4 = ((bf16[16,256,128]{2,1,0:T(8,128)(2,1)}), bf16[16,256,128]{2,1,0:T(8,128)(2,1)S(1)}, u32[]{:S(2)}, u32[]{:S(2)}) async-start(bf16[16,256,128]{2,1,0:T(8,128)(2,1)} %get-tuple-element.146), calls=%async_computation.4 | async-start | bytes 2097152 | tf_op jit(solution)/shard_map/all_to_all | solution.py:737
  20.3 10.9 %collective-permute-done.12.received_ref = bf16[256,768]{1,0:T(8,128)(2,1)S(1)} collective-permute-done((bf16[256,768]{1,0:T(8,128)(2,1)}, bf16[256,768]{1,0:T(8,128)(2,1)S(1)}, u32[]{:S(2)}, u32[]{:S(2)}) %collective-permute-start.12) | collective-permute-done | bytes 393248 | tf_op jit(solution)/shard_map/ppermute | solution.py:728
  31.2 2.8 %query_rows.1 = (bf16[256,768]{1,0:T(8,128)(2,1)S(1)}, bf16[256,768]{1,0:T(8,128)(2,1)}, bf16[256,768]{1,0:T(8,128)(2,1)}) custom-call(bf16[256,768]{1,0:T(8,128)(2,1)S(1)} %bitcast.39, bf16[256,768]{1,0:T(8,128)(2,1)S(1)} %collective-permute-done.12.received_ref, f32[768]{0:T(1024)S(1)} %copy-done.20, f32[768]{0:T(1024)S(1)} %copy-done.3, ...), custom_call_target="tpu_custom_call" | custom-call | flops 30000001024 | bytes 1048576 | tf_op jit(solution)/shard_map/query_rows/pallas_call | solution.py:576
  34.1 5.0 %all-to-all-done.4.own_ref = bf16[16,256,128]{2,1,0:T(8,128)(2,1)S(1)} async-done(((bf16[16,256,128]{2,1,0:T(8,128)(2,1)}), bf16[16,256,128]{2,1,0:T(8,128)(2,1)S(1)}, u32[]{:S(2)}, u32[]{:S(2)}) %all-to-all-start.4) | async-done | bytes 1048608 | tf_op jit(solution)/shard_map/all_to_all | solution.py:737
  39.1 0.5 collective-permute-start.16
  39.6 0.2 reduce-window.8
  39.8 0.1 pad_add_fusion
  39.9 0.1 select_reduce_fusion
  40.1 0.2 collective-permute-start.18
  40.3 2.2 collective-permute-done.15.peer_ref
  42.5 19.5 %attend.1 = (bf16[256,768]{1,0:T(8,128)(2,1)S(1)}, f32[2,64,1536]{2,1,0:T(8,128)}, f32[2,1,1536]{2,1,0:T(1,128)S(1)}) custom-call(s32[1]{0:T(128)} %bitcast.16.place_ref, bf16[256,768]{1,0:T(8,128)(2,1)} %get-tuple-element.149.query_ref, bf16[16,256,128]{2,1,0:T(8,128)(2,1)S(1)} %all-to-all-done.4.own_ref, ...), custom_call_target="tpu_custom_call" | custom-call | flops 24999999488 | bytes 8388608 | tf_op jit(solution)/shard_map/attend/pallas_call | solution.py:279
  62.0 1.5 residual.1
  63.6 0.4 collective-permute-start.17
  63.9 1.4 collective-permute-done.17.peer_ref
  65.3 8.3 %mlp.1 = (bf16[1536,768]{1,0:T(8,128)(2,1)}, bf16[768,1536]{1,0:T(8,128)(2,1)}, f32[1,1536]{1,0:T(1,128)}, f32[256,768]{1,0:T(8,128)}, bf16[256,768]{1,0:T(8,128...) custom-call(bf16[256,768]{1,0:T(8,128)(2,1)S(1)} %get-tuple-element.153.own_ref, ...), custom_call_target="tpu_custom_call" | custom-call | flops 10000000000 | bytes 1048576 | tf_op jit(solution)/shard_map/mlp/pallas_call | solution.py:576
  73.7 0.4 collective-permute-start.19
  74.2 1.3 collective-permute-done.19.peer_back_ref
  75.5 2.8 %residual_back.1 = (f32[256,768]{1,0:T(8,128)}, bf16[256,768]{1,0:T(8,128)(2,1)S(1)}, bf16[256,768]{1,0:T(8,128)(2,1)S(1)}, f32[8,768]{1,0:T(8,128)}) custom-call(f32[256,768]{1,0:T(8,128)S(1)} %get-tuple-element.157.back_ref, bf16[256,768]{1,0:T(8,128)(2,1)S(1)} %collective-permute-done.19.peer_back_ref, ...), custom_call_target="tpu_custom_call" | custom-call | flops 1000000000 | bytes 1048576 | tf_op jit(solution)/shard_map/residual_back/pallas_call | solution.py:576
  78.4 138.0 %conditional.1 = (bf16[1,256,768]{2,1,0:T(8,128)(2,1)}, f32[1,256,768]{2,1,0:T(8,128)}, f32[768]{0:T(1024)}, f32[768]{0:T(1024)}, f32[768,384]{1,0:T(8,128)}, /*...) conditional(s32[]{:T(128)} %bitcast.15, () %tuple.18, ...), branch_computations={%region_2.3_spmd, %region_3.6_spmd} | conditional | flops 56006414336 | bytes 75827368 | solution.py:883
  78.4 37.5 %attend_back.1 = (bf16[256,768]{1,0:T(8,128)(2,1)S(1)}, bf16[16,256,128]{2,1,0:T(8,128)(2,1)S(1)}, bf16[16,256,128]{2,1,0:T(8,128)(2,1)S(1)}) custom-call(s32[1]{0:T(128)} %get-tuple-element.50.place_ref, bf16[256,768]{1,0:T(8,128)(2,1)S(1)} %get-tuple-element.51.query_ref, bf16[16,256,128]{2,1,0:T(8,128)(2,1)S(1)} %get-tuple-element.52.own_ref, ...), custom_call_target="tpu_custom_call" | custom-call | flops 44999999488 | bytes 12582912 | tf_op jit(solution)/shard_map/cond/branch_1_fun/attend_back/pallas_call | solution.py:306
  115.9 0.6 collective-permute-start.2
  116.5 3.1 %query_back.1 = (f32[256,768]{1,0:T(8,128)S(1)}, f32[4608,128]{1,0:T(8,128)S(1)}, bf16[4608,128]{1,0:T(8,128)(2,1)}, f32[1,768]{1,0:T(1,128)S(1)}) custom-call(bf16[256,768]{1,0:T(8,128)(2,1)S(1)} %get-tuple-element.60.grad_ref, bf16[256,768]{1,0:T(8,128)(2,1)S(1)} %get-tuple-element.61.normed_ref, bf16[256,768]{1,0:T(8,128)(2,1)S(1)} %get-tuple-element.62.attended_ref, ...), custom_call_target="tpu_custom_call" | custom-call | flops 10000000000 | bytes 1048576 | tf_op jit(solution)/shard_map/cond/branch_1_fun/query_back/pallas_call | solution.py:576
  119.6 0.9 copy-done.12
  120.5 1.2 add_convert_fusion
  121.8 6.0 %all-to-all-start = ((bf16[16,256,128]{2,1,0:T(8,128)(2,1)}), bf16[16,256,128]{2,1,0:T(8,128)(2,1)}, u32[]{:S(2)}, u32[]{:S(2)}) async-start(bf16[16,256,128]{2,1,0:T(8,128)(2,1)} %add_convert_fusion), calls=%async_computation | async-start | bytes 2097152 | tf_op jit(solution)/shard_map/cond/branch_1_fun/all_to_all | solution.py:737
  127.8 1.0 pack.1
  128.9 0.8 copy-done
  129.7 3.2 %collective-permute-start.5 = (bf16[1152,128]{1,0:T(8,128)(2,1)}, bf16[1152,128]{1,0:T(8,128)(2,1)S(1)}, u32[]{:S(2)}, u32[]{:S(2)}) collective-permute-start(bf16[1152,128]{1,0:T(8,128)(2,1)} %get-tuple-element.80), channel_id=1, source_target_pairs={{0,64},{32,96},{64,0},{96,32},{1,65},{33,97},{65,1},{97,33},{2,66}... | collective-permute-start | bytes 884744 | tf_op jit(solution)/shard_map/cond/branch_1_fun/ppermute | solution.py:819
  132.9 0.7 collective-permute-start.6
  133.6 2.6 %collective-permute-start.7 = (bf16[1152,128]{1,0:T(8,128)(2,1)}, bf16[1152,128]{1,0:T(8,128)(2,1)S(1)}, u32[]{:S(2)}, u32[]{:S(2)}) collective-permute-start(bf16[1152,128]{1,0:T(8,128)(2,1)} %get-tuple-element.82), channel_id=1, source_target_pairs={{0,96},{32,0},{64,32},{96,64},{1,97},{33,1},{65,33},{97,65},{2,98}... | collective-permute-start | bytes 884744 | tf_op jit(solution)/shard_map/cond/branch_1_fun/ppermute | solution.py:819
  136.1 10.0 %all-to-all-done.arrived_ref = bf16[16,256,128]{2,1,0:T(8,128)(2,1)} async-done(((bf16[16,256,128]{2,1,0:T(8,128)(2,1)}), bf16[16,256,128]{2,1,0:T(8,128)(2,1)}, u32[]{:S(2)}, u32[]{:S(2)}) %all-to-all-start) | async-done | bytes 1048608 | tf_op jit(solution)/shard_map/cond/branch_1_fun/all_to_all | solution.py:737
  146.2 1.1 copy-done.13
  147.3 3.2 %token_back.1 = (f32[128,768]{1,0:T(8,128)S(1)}, bf16[128,768]{1,0:T(8,128)(2,1)S(1)}, bf16[1024,128]{1,0:T(8,128)(2,1)}) custom-call(bf16[16,256,128]{2,1,0:T(8,128)(2,1)} %all-to-all-done.arrived_ref, f32[256,768]{1,0:T(8,128)S(1)} %copy-done.13, bf16[768,128]{1,0:T(8,128)(2,1)} %get-tuple-element.67.weight_ref, bf16[256,768]{1,0:T(8,128)(2,1)} %copy-done.25, ...), custom_call_target="tpu_custom_call" | custom-call | flops 1000000000 | bytes 1048576 | tf_op jit(solution)/shard_map/cond/branch_1_fun/token_back/pallas_call | solution.py:576
  150.6 4.6 %all-to-all-start.1 = ((bf16[4,256,128]{2,1,0:T(8,128)(2,1)}), bf16[4,256,128]{2,1,0:T(8,128)(2,1)S(1)}, u32[]{:S(2)}, u32[]{:S(2)}) async-start(bf16[4,256,128]{2,1,0:T(8,128)(2,1)} %bitcast.4), calls=%async_computation.1 | async-start | bytes 524288 | tf_op jit(solution)/shard_map/cond/branch_1_fun/all_to_all | solution.py:737
  155.1 0.1 add_convert_fusion.2
  155.3 6.7 %all-to-all-done.1 = bf16[4,256,128]{2,1,0:T(8,128)(2,1)S(1)} async-done(((bf16[4,256,128]{2,1,0:T(8,128)(2,1)}), bf16[4,256,128]{2,1,0:T(8,128)(2,1)S(1)}, u32[]{:S(2)}, u32[]{:S(2)}) %all-to-all-start.1) | async-done | bytes 262176 | tf_op jit(solution)/shard_map/cond/branch_1_fun/all_to_all | solution.py:737
  162.0 0.8 pad_maximum_fusion
  162.8 3.5 %all-to-all-start.2 = ((bf16[16,88,128]{2,1,0:T(8,128)(2,1)}), bf16[16,88,128]{2,1,0:T(8,128)(2,1)S(1)}, u32[]{:S(2)}, u32[]{:S(2)}) async-start(bf16[16,88,128]{2,1,0:T(8,128)(2,1)} %pad_maximum_fusion), calls=%async_computation.2 | async-start | bytes 720896 | tf_op jit(solution)/shard_map/cond/branch_1_fun/all_to_all | solution.py:737
  166.3 0.1 collective-permute-start
  166.4 9.1 %all-to-all-done.2 = bf16[16,88,128]{2,1,0:T(8,128)(2,1)S(1)} async-done(((bf16[16,88,128]{2,1,0:T(8,128)(2,1)}), bf16[16,88,128]{2,1,0:T(8,128)(2,1)S(1)}, u32[]{:S(2)}, u32[]{:S(2)}) %all-to-all-start.2) | async-done | bytes 360480 | tf_op jit(solution)/shard_map/cond/branch_1_fun/all_to_all | solution.py:737
  175.6 0.1 collective-permute-start.8
  175.7 1.1 collective-permute-done.8
  176.9 0.8 broadcast_in_dim.22
  177.7 3.5 %all-to-all-start.3 = ((bf16[16,88,128]{2,1,0:T(8,128)(2,1)}), bf16[16,88,128]{2,1,0:T(8,128)(2,1)S(1)}, u32[]{:S(2)}, u32[]{:S(2)}) async-start(bf16[16,88,128]{2,1,0:T(8,128)(2,1)} %broadcast_in_dim.22), calls=%async_computation.3 | async-start | bytes 720896 | tf_op jit(solution)/shard_map/cond/branch_1_fun/all_to_all | solution.py:737
  181.3 0.1 add_convert_fusion.1
  181.5 4.8 %collective-permute-start.1 = (bf16[128,768]{1,0:T(8,128)(2,1)S(1)}, bf16[128,768]{1,0:T(8,128)(2,1)S(1)}, u32[]{:S(2)}, u32[]{:S(2)}) collective-permute-start(bf16[128,768]{1,0:T(8,128)(2,1)S(1)} %get-tuple-element.190), channel_id=1, source_target_pairs={{0,31},{1,30},{2,29},{3,28},{4,27},{5,26},{6,25},{7,24},{8,23},{9,... | collective-permute-start | bytes 589832 | tf_op jit(solution)/shard_map/cond/branch_1_fun/ppermute | solution.py:728
  186.3 6.7 %all-to-all-done.3.own_ref = bf16[16,88,128]{2,1,0:T(8,128)(2,1)S(1)} async-done(((bf16[16,88,128]{2,1,0:T(8,128)(2,1)}), bf16[16,88,128]{2,1,0:T(8,128)(2,1)S(1)}, u32[]{:S(2)}, u32[]{:S(2)}) %all-to-all-start.3) | async-done | bytes 360480 | tf_op jit(solution)/shard_map/cond/branch_1_fun/all_to_all | solution.py:737
  193.0 1.4 collective-permute-start.11
  194.3 1.7 collective-permute-start.10
  196.1 1.6 collective-permute-done.1
  197.6 0.8 maximum_bitcast_fusion.1
  198.4 6.7 %collective-permute-done.3 = bf16[128,768]{1,0:T(8,128)(2,1)S(1)} collective-permute-done((bf16[128,768]{1,0:T(8,128)(2,1)S(1)}, bf16[128,768]{1,0:T(8,128)(2,1)S(1)}, u32[]{:S(2)}, u32[]{:S(2)}) %collective-permute-start.3) | collective-permute-done | bytes 196640 | tf_op jit(solution)/shard_map/cond/branch_1_fun/ppermute | solution.py:728
  205.1 0.9 maximum_bitcast_fusion
  206.0 1.2 collective-permute-done.10.second_ref
  207.2 5.5 %collective-permute-done.9.first_ref = bf16[16,88,128]{2,1,0:T(8,128)(2,1)S(1)} collective-permute-done((bf16[16,88,128]{2,1,0:T(8,128)(2,1)S(1)}, bf16[16,88,128]{2,1,0:T(8,128)(2,1)S(1)}, u32[]{:S(2)}, u32[]{:S(2)}) %collective-permute-start.9) | collective-permute-done | bytes 360480 | tf_op jit(solution)/shard_map/cond/branch_1_fun/ppermute | solution.py:844
  212.7 1.8 unpack.1
  214.6 0.6 slice_bitcast_fusion.7
  215.1 0.6 select_bitcast_fusion
  215.7 0.6 slice_bitcast_fusion.1
  216.3 14.6 %all-reduce.3.cloned.1.call-done = (bf16[1536,768]{1,0:T(8,128)(2,1)}, bf16[768,1536]{1,0:T(8,128)(2,1)}) async-done(((bf16[1536,768]{1,0:T(8,128)(2,1)}, bf16[768,1536]{1,0:T(8,128)(2,1)}), (bf16[1536,768]{1,0:T(8,128)(2,1)}, bf16[768,1536]{1,0:T(8,128)(2,1)})) %all-reduce.3.cloned.1.call-update) | async-done | bytes 4718608 | tf_op jit(solution)/shard_map/psum | solution.py:796
  230.9 5.5 %widen.1 = (f32[1536,768]{1,0:T(8,128)}, f32[768,1536]{1,0:T(8,128)}) custom-call(bf16[1536,768]{1,0:T(8,128)(2,1)} %get-tuple-element.187.contract_ref, bf16[768,1536]{1,0:T(8,128)(2,1)} %get-tuple-element.188.expand_ref), custom_call_target="tpu_custom_call" | custom-call | tf_op jit(solution)/shard_map/widen/pallas_call | solution.py:640
  (97 shorter events, 0.7 us)
Async XLA Ops:
  7.2 24.0 %copy-start.20 = (f32[768]{0:T(1024)S(1)}, f32[768]{0:T(1024)}, u32[]{:S(2)}) copy-start(f32[768]{0:T(1024)} %gain_ref.5) | copy-start | bytes 9220
  7.2 24.0 %copy-start.3 = (f32[768]{0:T(1024)S(1)}, f32[768]{0:T(1024)}, u32[]{:S(2)}) copy-start(f32[768]{0:T(1024)} %shift_ref.4) | copy-start | bytes 9220
  7.2 24.0 %copy-start.2 = (bf16[1,256,768]{2,1,0:T(8,128)(2,1)S(1)}, bf16[1,256,768]{2,1,0:T(8,128)(2,1)}, u32[]{:S(2)}) copy-start(bf16[1,256,768]{2,1,0:T(8,128)(2,1)} %param.19) | copy-start | bytes 1179652
  7.2 24.0 %copy-start.11 = (f32[384]{0:T(512)S(1)}, f32[384]{0:T(512)}, u32[]{:S(2)}) copy-start(f32[384]{0:T(512)} %mine_bias_ref.1) | copy-start | bytes 4612
  7.2 24.0 %collective-permute-start.13 = (bf16[768,384]{1,0:T(8,128)(2,1)}, bf16[768,384]{1,0:T(8,128)(2,1)}, u32[]{:S(2)}, u32[]{:S(2)}) collective-permute-start(bf16[768,384]{1,0:T(8,128)(2,1)} %mine_ref.3), channel_id=1, source_target_pairs={{0,1},{1,0},{2,3},{3,2},{4,5},{5,4},{6,7},{7,6},{8,9},{9,8},{10,11... | collective-permute-start | bytes 1769480 | tf_op jit(solution)/shard_map/ppermute | solution.py:723
  10.1 21.1 %collective-permute-start.12 = (bf16[256,768]{1,0:T(8,128)(2,1)}, bf16[256,768]{1,0:T(8,128)(2,1)S(1)}, u32[]{:S(2)}, u32[]{:S(2)}) collective-permute-start(bf16[256,768]{1,0:T(8,128)(2,1)} %get-tuple-element.147), channel_id=1, source_target_pairs={{0,31},{1,30},{2,29},{3,28},{4,27},{5,26},{6,25},{7,24},{8,23},{9,... | collective-permute-start | bytes 1179656 | tf_op jit(solution)/shard_map/ppermute | solution.py:728
  16.5 3.8 %collective-permute-start.14 = (f32[384]{0:T(512)}, f32[384]{0:T(512)S(1)}, u32[]{:S(2)}, u32[]{:S(2)}) collective-permute-start(f32[384]{0:T(512)} %mine_bias_ref.1), channel_id=1, source_target_pairs={{0,1},{1,0},{2,3},{3,2},{4,5},{5,4},{6,7},{7,6},{8,9},{9,8},{10,11... | collective-permute-start | bytes 4616 | tf_op jit(solution)/shard_map/ppermute | solution.py:723
  16.5 22.5 %all-to-all-start.4 = ((bf16[16,256,128]{2,1,0:T(8,128)(2,1)}), bf16[16,256,128]{2,1,0:T(8,128)(2,1)S(1)}, u32[]{:S(2)}, u32[]{:S(2)}) async-start(bf16[16,256,128]{2,1,0:T(8,128)(2,1)} %get-tuple-element.146), calls=%async_computation.4 | async-start | bytes 2097152 | tf_op jit(solution)/shard_map/all_to_all | solution.py:737
  20.2 18.9 %copy-start.6 = (bf16[384,768]{1,0:T(8,128)(2,1)S(1)}, bf16[384,768]{1,0:T(8,128)(2,1)}, u32[]{:S(2)}) copy-start(bf16[384,768]{1,0:T(8,128)(2,1)} %mine_ref.5) | copy-start | bytes 1769476
  20.2 19.4 %copy-start.24 = (s32[1,8]{1,0:T(1,128)S(1)}, s32[1,8]{1,0:T(1,128)}, u32[]{:S(2)}) copy-start(s32[1,8]{1,0:T(1,128)} %param.35) | copy-start | bytes 100
  20.2 19.8 %copy-start.16 = (bf16[1,256,768]{2,1,0:T(8,128)(2,1)S(1)}, bf16[1,256,768]{2,1,0:T(8,128)(2,1)}, u32[]{:S(2)}) copy-start(bf16[1,256,768]{2,1,0:T(8,128)(2,1)} %param.34) | copy-start | bytes 1179652
  20.2 210.7 %all-reduce.3.cloned.1.call-start = ((), (), s32[]{:S(2)}) async-start(), calls=%async_computation.5 | async-start | bytes 9437184 | tf_op jit(solution)/shard_map/psum | solution.py:796
  39.1 22.9 %copy-start.14 = (bf16[16,256,128]{2,1,0:T(8,128)(2,1)}, bf16[16,256,128]{2,1,0:T(8,128)(2,1)S(1)}, u32[]{:S(2)}) copy-start(bf16[16,256,128]{2,1,0:T(8,128)(2,1)S(1)} %all-to-all-done.4.own_ref) | copy-start | bytes 3145732
  39.1 3.4 %collective-permute-start.15 = (bf16[16,256,128]{2,1,0:T(8,128)(2,1)S(1)}, bf16[16,256,128]{2,1,0:T(8,128)(2,1)}, u32[]{:S(2)}, u32[]{:S(2)}) collective-permute-start(bf16[16,256,128]{2,1,0:T(8,128)(2,1)S(1)} %all-to-all-done.4.own_ref), channel_id=1, source_target_pairs={{0,1},{1,0},{2,3},{3,2},{4,5},{5,4},{6,7},{7,6},{8,9},{9,8},{10,11... | collective-permute-start | bytes 3145736 | tf_op jit(solution)/shard_map/ppermute | solution.py:723
  39.1 22.9 %collective-permute-start.16 = (bf16[384,768]{1,0:T(8,128)(2,1)S(1)}, bf16[384,768]{1,0:T(8,128)(2,1)S(1)}, u32[]{:S(2)}, u32[]{:S(2)}) collective-permute-start(bf16[384,768]{1,0:T(8,128)(2,1)S(1)} %copy-done.6), channel_id=1, source_target_pairs={{0,1},{1,0},{2,3},{3,2},{4,5},{5,4},{6,7},{7,6},{8,9},{9,8},{10,11... | collective-permute-start | bytes 1769480 | tf_op jit(solution)/shard_map/ppermute | solution.py:723
  40.1 23.8 %collective-permute-start.18 = (bf16[256,768]{1,0:T(8,128)(2,1)S(1)}, bf16[256,768]{1,0:T(8,128)(2,1)S(1)}, u32[]{:S(2)}, u32[]{:S(2)}) collective-permute-start(bf16[256,768]{1,0:T(8,128)(2,1)S(1)} %pad_maximum_fusion.2.own_grad_ref.grad_ref), channel_id=1, source_target_pairs={{0,1},{1,0},{2,3},{3,2},{4,5},{5,4},{6,7},{7,6},{8,9},{9,8},{10,11... | collective-permute-start | bytes 1179656 | tf_op jit(solution)/shard_map/ppermute | solution.py:723
  42.5 19.5 %copy-start.8 = (f32[768]{0:T(1024)S(1)}, f32[768]{0:T(1024)}, u32[]{:S(2)}) copy-start(f32[768]{0:T(1024)} %bias_ref.4) | copy-start | bytes 9220
  42.5 19.5 %copy-start.9 = (f32[768]{0:T(1024)S(1)}, f32[768]{0:T(1024)}, u32[]{:S(2)}) copy-start(f32[768]{0:T(1024)} %shift_ref.5) | copy-start | bytes 9220
  42.5 19.5 %copy-start.10 = (f32[768]{0:T(1024)S(1)}, f32[768]{0:T(1024)}, u32[]{:S(2)}) copy-start(f32[768]{0:T(1024)} %gain_ref.7) | copy-start | bytes 9220
  42.5 22.8 %copy-start.5 = (bf16[1536,768]{1,0:T(8,128)(2,1)S(1)}, bf16[1536,768]{1,0:T(8,128)(2,1)}, u32[]{:S(2)}) copy-start(bf16[1536,768]{1,0:T(8,128)(2,1)} %contract_ref.1) | copy-start | bytes 7077892
  62.0 2.0 copy-start.29
  62.0 3.3 %copy-start.4 = (bf16[768,1536]{1,0:T(8,128)(2,1)S(1)}, bf16[768,1536]{1,0:T(8,128)(2,1)}, u32[]{:S(2)}) copy-start(bf16[768,1536]{1,0:T(8,128)(2,1)} %expand_ref.1) | copy-start | bytes 7077892
  62.0 3.3 %copy-start.7 = (f32[1536]{0:T(1024)S(1)}, f32[1536]{0:T(1024)}, u32[]{:S(2)}) copy-start(f32[1536]{0:T(1024)} %bias_ref.5) | copy-start | bytes 18436
  63.6 1.7 collective-permute-start.17
  73.6 4.7 %copy-start.15 = (bf16[16,256,128]{2,1,0:T(8,128)(2,1)S(1)}, bf16[16,256,128]{2,1,0:T(8,128)(2,1)}, u32[]{:S(2)}) copy-start(bf16[16,256,128]{2,1,0:T(8,128)(2,1)} %copy-done.14) | copy-start | bytes 3145732
  73.7 4.7 %copy-start.22 = (bf16[768,384]{1,0:T(8,128)(2,1)S(1)}, bf16[768,384]{1,0:T(8,128)(2,1)}, u32[]{:S(2)}) copy-start(bf16[768,384]{1,0:T(8,128)(2,1)} %mine_ref.3) | copy-start | bytes 1769476
  73.7 4.7 %copy-start.26 = (bf16[256,768]{1,0:T(8,128)(2,1)S(1)}, bf16[256,768]{1,0:T(8,128)(2,1)}, u32[]{:S(2)}) copy-start(bf16[256,768]{1,0:T(8,128)(2,1)} %get-tuple-element.162) | copy-start | bytes 1179652
  73.7 4.7 %copy-start.30 = (bf16[256,768]{1,0:T(8,128)(2,1)S(1)}, bf16[256,768]{1,0:T(8,128)(2,1)}, u32[]{:S(2)}) copy-start(bf16[256,768]{1,0:T(8,128)(2,1)} %copy-done.29) | copy-start | bytes 1179652
  73.7 4.7 %copy-start.31 = (f32[2,64,1536]{2,1,0:T(8,128)S(1)}, f32[2,64,1536]{2,1,0:T(8,128)}, u32[]{:S(2)}) copy-start(f32[2,64,1536]{2,1,0:T(8,128)} %get-tuple-element.160) | copy-start | bytes 2359300
  73.7 4.7 %copy-start.32 = (bf16[256,768]{1,0:T(8,128)(2,1)S(1)}, bf16[256,768]{1,0:T(8,128)(2,1)}, u32[]{:S(2)}) copy-start(bf16[256,768]{1,0:T(8,128)(2,1)} %get-tuple-element.149.query_ref) | copy-start | bytes 1179652
  73.7 1.8 collective-permute-start.19
  78.4 37.5 %copy-start.25 = (bf16[256,768]{1,0:T(8,128)(2,1)}, bf16[256,768]{1,0:T(8,128)(2,1)S(1)}, u32[]{:S(2)}) copy-start(bf16[256,768]{1,0:T(8,128)(2,1)S(1)} %get-tuple-element.68.tokens_ref) | copy-start | bytes 1179652 | tf_op jit(solution)/shard_map/cond
  78.4 38.1 %copy-start.27 = (bf16[256,768]{1,0:T(8,128)(2,1)}, bf16[256,768]{1,0:T(8,128)(2,1)S(1)}, u32[]{:S(2)}) copy-start(bf16[256,768]{1,0:T(8,128)(2,1)S(1)} %get-tuple-element.61.normed_ref) | copy-start | bytes 1179652 | tf_op jit(solution)/shard_map/cond
  115.9 4.6 %collective-permute-start.2 = (bf16[16,256,128]{2,1,0:T(8,128)(2,1)S(1)}, bf16[16,256,128]{2,1,0:T(8,128)(2,1)S(1)}, u32[]{:S(2)}, u32[]{:S(2)}) collective-permute-start(bf16[16,256,128]{2,1,0:T(8,128)(2,1)S(1)} %get-tuple-element.59), channel_id=1, source_target_pairs={{0,1},{1,0},{2,3},{3,2},{4,5},{5,4},{6,7},{7,6},{8,9},{9,8},{10,11... | collective-permute-start | bytes 3145736 | tf_op jit(solution)/shard_map/cond/branch_1_fun/ppermute | solution.py:723
  119.6 0.9 copy-start.12
  120.5 7.4 %collective-permute-start.4 = (bf16[4608,128]{1,0:T(8,128)(2,1)}, bf16[4608,128]{1,0:T(8,128)(2,1)S(1)}, u32[]{:S(2)}, u32[]{:S(2)}) collective-permute-start(bf16[4608,128]{1,0:T(8,128)(2,1)} %get-tuple-element.77), channel_id=1, source_target_pairs={{0,1},{1,0},{2,3},{3,2},{4,5},{5,4},{6,7},{7,6},{8,9},{9,8},{10,11... | collective-permute-start | bytes 3538952 | tf_op jit(solution)/shard_map/cond/branch_1_fun/ppermute | solution.py:723
  121.8 24.4 %all-to-all-start = ((bf16[16,256,128]{2,1,0:T(8,128)(2,1)}), bf16[16,256,128]{2,1,0:T(8,128)(2,1)}, u32[]{:S(2)}, u32[]{:S(2)}) async-start(bf16[16,256,128]{2,1,0:T(8,128)(2,1)} %add_convert_fusion), calls=%async_computation | async-start | bytes 2097152 | tf_op jit(solution)/shard_map/cond/branch_1_fun/all_to_all | solution.py:737
  127.8 18.4 %copy-start.28 = (f32[1,1536]{1,0:T(1,128)S(1)}, f32[1,1536]{1,0:T(1,128)}, u32[]{:S(2)}) copy-start(f32[1,1536]{1,0:T(1,128)} %get-tuple-element.73.expand_bias_ref) | copy-start | bytes 18436 | tf_op jit(solution)/shard_map/cond
  128.9 0.8 copy-start
  129.7 20.9 %collective-permute-start.5 = (bf16[1152,128]{1,0:T(8,128)(2,1)}, bf16[1152,128]{1,0:T(8,128)(2,1)S(1)}, u32[]{:S(2)}, u32[]{:S(2)}) collective-permute-start(bf16[1152,128]{1,0:T(8,128)(2,1)} %get-tuple-element.80), channel_id=1, source_target_pairs={{0,64},{32,96},{64,0},{96,32},{1,65},{33,97},{65,1},{97,33},{2,66}... | collective-permute-start | bytes 884744 | tf_op jit(solution)/shard_map/cond/branch_1_fun/ppermute | solution.py:819
  132.9 17.7 %collective-permute-start.6 = (bf16[1152,128]{1,0:T(8,128)(2,1)}, bf16[1152,128]{1,0:T(8,128)(2,1)S(1)}, u32[]{:S(2)}, u32[]{:S(2)}) collective-permute-start(bf16[1152,128]{1,0:T(8,128)(2,1)} %get-tuple-element.81), channel_id=1, source_target_pairs={{0,32},{32,64},{64,96},{96,0},{1,33},{33,65},{65,97},{97,1},{2,34}... | collective-permute-start | bytes 884744 | tf_op jit(solution)/shard_map/cond/branch_1_fun/ppermute | solution.py:819
  133.6 17.0 %collective-permute-start.7 = (bf16[1152,128]{1,0:T(8,128)(2,1)}, bf16[1152,128]{1,0:T(8,128)(2,1)S(1)}, u32[]{:S(2)}, u32[]{:S(2)}) collective-permute-start(bf16[1152,128]{1,0:T(8,128)(2,1)} %get-tuple-element.82), channel_id=1, source_target_pairs={{0,96},{32,0},{64,32},{96,64},{1,97},{33,1},{65,33},{97,65},{2,98}... | collective-permute-start | bytes 884744 | tf_op jit(solution)/shard_map/cond/branch_1_fun/ppermute | solution.py:819
  146.2 1.1 copy-start.13
  147.3 7.9 %copy-start.1 = (f32[1152,128]{1,0:T(8,128)S(1)}, f32[1152,128]{1,0:T(8,128)}, u32[]{:S(2)}) copy-start(f32[1152,128]{1,0:T(8,128)} %copy-done) | copy-start | bytes 1769476 | tf_op jit(solution)/shard_map/cond
  150.5 15.8 %copy-start.23 = (bf16[256,768]{1,0:T(8,128)(2,1)S(1)}, bf16[256,768]{1,0:T(8,128)(2,1)}, u32[]{:S(2)}) copy-start(bf16[256,768]{1,0:T(8,128)(2,1)} %get-tuple-element.48) | copy-start | bytes 1179652 | tf_op jit(solution)/shard_map/cond
  150.6 11.4 %all-to-all-start.1 = ((bf16[4,256,128]{2,1,0:T(8,128)(2,1)}), bf16[4,256,128]{2,1,0:T(8,128)(2,1)S(1)}, u32[]{:S(2)}, u32[]{:S(2)}) async-start(bf16[4,256,128]{2,1,0:T(8,128)(2,1)} %bitcast.4), calls=%async_computation.1 | async-start | bytes 524288 | tf_op jit(solution)/shard_map/cond/branch_1_fun/all_to_all | solution.py:737
  155.3 26.0 %copy-start.17 = (f32[256,768]{1,0:T(8,128)S(1)}, f32[256,768]{1,0:T(8,128)}, u32[]{:S(2)}) copy-start(f32[256,768]{1,0:T(8,128)} %get-tuple-element.46) | copy-start | bytes 2359300 | tf_op jit(solution)/shard_map/cond
  155.3 26.0 %copy-start.18 = (f32[256,768]{1,0:T(8,128)S(1)}, f32[256,768]{1,0:T(8,128)}, u32[]{:S(2)}) copy-start(f32[256,768]{1,0:T(8,128)} %get-tuple-element.47) | copy-start | bytes 2359300 | tf_op jit(solution)/shard_map/cond
  155.3 26.0 %copy-start.21 = (f32[768]{0:T(1024)S(1)}, f32[768]{0:T(1024)}, u32[]{:S(2)}) copy-start(f32[768]{0:T(1024)} %get-tuple-element.186) | copy-start | bytes 9220 | tf_op jit(solution)/shard_map/cond
  162.8 12.7 %all-to-all-start.2 = ((bf16[16,88,128]{2,1,0:T(8,128)(2,1)}), bf16[16,88,128]{2,1,0:T(8,128)(2,1)S(1)}, u32[]{:S(2)}, u32[]{:S(2)}) async-start(bf16[16,88,128]{2,1,0:T(8,128)(2,1)} %pad_maximum_fusion), calls=%async_computation.2 | async-start | bytes 720896 | tf_op jit(solution)/shard_map/cond/branch_1_fun/all_to_all | solution.py:737
  166.3 14.9 %collective-permute-start = (bf16[256,768]{1,0:T(8,128)(2,1)S(1)}, bf16[256,768]{1,0:T(8,128)(2,1)S(1)}, u32[]{:S(2)}, u32[]{:S(2)}) collective-permute-start(bf16[256,768]{1,0:T(8,128)(2,1)S(1)} %copy-done.23), channel_id=1, source_target_pairs={{0,1},{1,0},{2,3},{3,2},{4,5},{5,4},{6,7},{7,6},{8,9},{9,8},{10,11... | collective-permute-start | bytes 1179656 | tf_op jit(solution)/shard_map/cond/branch_1_fun/ppermute | solution.py:723
  175.6 1.3 collective-permute-start.8
  177.7 15.3 %all-to-all-start.3 = ((bf16[16,88,128]{2,1,0:T(8,128)(2,1)}), bf16[16,88,128]{2,1,0:T(8,128)(2,1)S(1)}, u32[]{:S(2)}, u32[]{:S(2)}) async-start(bf16[16,88,128]{2,1,0:T(8,128)(2,1)} %broadcast_in_dim.22), calls=%async_computation.3 | async-start | bytes 720896 | tf_op jit(solution)/shard_map/cond/branch_1_fun/all_to_all | solution.py:737
  181.5 16.2 %collective-permute-start.1 = (bf16[128,768]{1,0:T(8,128)(2,1)S(1)}, bf16[128,768]{1,0:T(8,128)(2,1)S(1)}, u32[]{:S(2)}, u32[]{:S(2)}) collective-permute-start(bf16[128,768]{1,0:T(8,128)(2,1)S(1)} %get-tuple-element.190), channel_id=1, source_target_pairs={{0,31},{1,30},{2,29},{3,28},{4,27},{5,26},{6,25},{7,24},{8,23},{9,... | collective-permute-start | bytes 589832 | tf_op jit(solution)/shard_map/cond/branch_1_fun/ppermute | solution.py:728
  193.0 13.1 %collective-permute-start.11 = (bf16[16,88,128]{2,1,0:T(8,128)(2,1)S(1)}, bf16[16,88,128]{2,1,0:T(8,128)(2,1)S(1)}, u32[]{:S(2)}, u32[]{:S(2)}) collective-permute-start(bf16[16,88,128]{2,1,0:T(8,128)(2,1)S(1)} %all-to-all-done.3.own_ref), channel_id=1, source_target_pairs={{0,96},{32,0},{64,32},{96,64},{1,97},{33,1},{65,33},{97,65},{2,98}... | collective-permute-start | bytes 1081352 | tf_op jit(solution)/shard_map/cond/branch_1_fun/ppermute | solution.py:844
  194.3 12.9 %collective-permute-start.10 = (bf16[16,88,128]{2,1,0:T(8,128)(2,1)S(1)}, bf16[16,88,128]{2,1,0:T(8,128)(2,1)S(1)}, u32[]{:S(2)}, u32[]{:S(2)}) collective-permute-start(bf16[16,88,128]{2,1,0:T(8,128)(2,1)S(1)} %all-to-all-done.3.own_ref), channel_id=1, source_target_pairs={{0,64},{32,96},{64,0},{96,32},{1,65},{33,97},{65,1},{97,33},{2,66}... | collective-permute-start | bytes 1081352 | tf_op jit(solution)/shard_map/cond/branch_1_fun/ppermute | solution.py:844
  196.1 16.7 %collective-permute-start.9 = (bf16[16,88,128]{2,1,0:T(8,128)(2,1)S(1)}, bf16[16,88,128]{2,1,0:T(8,128)(2,1)S(1)}, u32[]{:S(2)}, u32[]{:S(2)}) collective-permute-start(bf16[16,88,128]{2,1,0:T(8,128)(2,1)S(1)} %all-to-all-done.3.own_ref), channel_id=1, source_target_pairs={{0,32},{32,64},{64,96},{96,0},{1,33},{33,65},{65,97},{97,1},{2,34}... | collective-permute-start | bytes 1081352 | tf_op jit(solution)/shard_map/cond/branch_1_fun/ppermute | solution.py:844
  196.1 9.0 %collective-permute-start.3 = (bf16[128,768]{1,0:T(8,128)(2,1)S(1)}, bf16[128,768]{1,0:T(8,128)(2,1)S(1)}, u32[]{:S(2)}, u32[]{:S(2)}) collective-permute-start(bf16[128,768]{1,0:T(8,128)(2,1)S(1)} %get-tuple-element.75), channel_id=1, source_target_pairs={{0,31},{1,30},{2,29},{3,28},{4,27},{5,26},{6,25},{7,24},{8,23},{9,... | collective-permute-start | bytes 589832 | tf_op jit(solution)/shard_map/cond/branch_1_fun/ppermute | solution.py:728
  216.3 20.1 %copy-start.19 = (f32[1536]{0:T(1024)}, f32[1536]{0:T(1024)S(1)}, u32[]{:S(2)}) copy-start(f32[1536]{0:T(1024)S(1)} %get-tuple-element.143) | copy-start | bytes 18436
Sparse Core Ops, SparseCore 0:
  73.8 157.1 all-reduce.2

commit v2 on v1

--- a/solution.py
+++ b/solution.py
@@ -40,18 +40,17 @@
     return jnp.concatenate([mask, mask], axis=1)
 
 
-def in_pairs(first, last, step):
-    count = jnp.maximum(last - first, 0)
-
-    def two(i, _):
-        step(first + 2 * i, 2)
-        return 0
-
-    lax.fori_loop(0, lax.div(count, 2), two, 0)
-
-    @pl.when(lax.rem(count, 2) == 1)
-    def _():
-        step(last - 1, 1)
+def in_groups(first, last, step, sizes):
+    at = first
+    for size in sizes:
+        count = lax.div(jnp.maximum(last - at, 0), size)
+
+        def group(i, _, at=at, size=size):
+            step(at + size * i, size)
+            return 0
+
+        lax.fori_loop(0, count, group, 0)
+        at = at + size * count
 
 
 def block_of(own_ref, peer_ref, place, tile):
@@ -132,7 +131,9 @@
                 set_shift(True)
                 mask = mask_of(0, first, starts)
                 gather(0, exps([v + mask for v in scores(0)]))
-                in_pairs(1, diag, lambda tile, count: gather(tile, exps(scores(tile, count)), count=count))
+                in_groups(
+                    1, diag, lambda tile, count: gather(tile, exps(scores(tile, count)), count=count), (4, 2, 1)
+                )
 
         sweep(False)
 
@@ -245,7 +246,7 @@
                 qt[c, DH : DH + 16, cols] = pieces(jnp.where(starts <= TILE, log_ref[c, :, cols], -NEG), LANES)
             add(0, mask_of(0, first, starts_ref[c]))
 
-            in_pairs(1, diag, lambda tile, count: add(tile, count=count))
+            in_groups(1, diag, lambda tile, count: add(tile, count=count), (2, 1))
 
         for s in range(subs):
             cols = slice(s * LANES, (s + 1) * LANES)
@@ -292,7 +293,7 @@
             pltpu.VMEM((2, DH + 16, lanes), jnp.float32),
             pltpu.VMEM((2, 8, lanes), jnp.float32),
         ],
-        compiler_params=pltpu.CompilerParams(vmem_limit_bytes=16 * 2**20),
+        compiler_params=pltpu.CompilerParams(vmem_limit_bytes=28 * 2**20),
         cost_estimate=pl.CostEstimate(flops=25 * 10**9, bytes_accessed=8 * 2**20, transcendentals=13 * 10**6),
         name="attend",
     )(place, query8, own, peer, starts)

time: 244 us -> 243 us (level)
  no operation moved by 1% of the time
where the time goes in v2:
time: 243 us; the launch traced here: 242 us
  Pallas kernels  89.1 us (37%)
  waiting for transfers between devices  83.7 us (34%)
  starting transfers between devices  44.3 us (18%)
  between operations  14.3 us (6%)
  other arithmetic  5.22 us (2%)
  local copies, waits for them, and re-layouts  5.03 us (2%)
    all_to_all x5, waiting for transfers between devices, spread_out(): return lax.all_to_all(blocks, axis, split_axis=0, concat_axis=0, tiled=True)  37.5 us
    pallas_call x1, Pallas kernels, attend_back(): pl.pallas_call(backward_kernel, out_shape=(jax.ShapeDtypeStruct((rows, wi...  37.5 us
    pallas_call x7, Pallas kernels, run(): pl.pallas_call(kernel, out_shape=outs, in_specs=[VM] * len(args), out_spe...  24.7 us
    all_to_all x5, starting transfers between devices, spread_out(): return lax.all_to_all(blocks, axis, split_axis=0, concat_axis=0, tiled=True)  21.5 us
    ppermute x3, waiting for transfers between devices, opposite(): lax.ppermute(value, ('seq', 'heads'), [(i, count - 1 - i) for i in range(...  19.2 us
    pallas_call x1, Pallas kernels, attend(): pl.pallas_call(forward_kernel, out_shape=(jax.ShapeDtypeStruct((rows, wid...  18.6 us
    psum x1, waiting for transfers between devices, per_device(): lax.psum((contract_part, expand_part), ('win', 'seq'))  14.1 us
    ppermute x3, starting transfers between devices, opposite(): lax.ppermute(value, ('seq', 'heads'), [(i, count - 1 - i) for i in range(...  11.2 us
  transfers between devices with their start and end apart: 26, of which 15 were waited for; matrix products, arithmetic and copies ran while one was open for 3% of the time, Pallas kernels for 31%

profile of v2, /device:TPU:0, one launch (start us, length us, event | category | flops | bytes accessed | tf_op | source)
XLA Modules:
  0.0 242.0 jit_solution(8132396442378296900)
XLA Ops:
  7.2 0.1 collective-permute-start.13
  7.3 2.8 %own_keyval.1 = (bf16[16,256,128]{2,1,0:T(8,128)(2,1)}, bf16[256,768]{1,0:T(8,128)(2,1)}) custom-call(bf16[256,768]{1,0:T(8,128)(2,1)} %bitcast.38, bf16[256,768]{1,0:T(8,128)(2,1)} %bitcast.41, f32[768]{0:T(1024)} %gain_ref.5, f32[768]{0:T(1024)} %shift_ref.4, bf16[768,128]{1,0:T(8,128)(2,1)} %weight_ref.1, f32[64]{0:T(128)} %bias_ref.3), custom_call_target="tpu_custom_call" | custom-call | flops 100000000 | bytes 1048576 | tf_op jit(solution)/shard_map/own_keyval/pallas_call | solution.py:577
  10.1 6.4 %collective-permute-start.12 = (bf16[256,768]{1,0:T(8,128)(2,1)}, bf16[256,768]{1,0:T(8,128)(2,1)S(1)}, u32[]{:S(2)}, u32[]{:S(2)}) collective-permute-start(bf16[256,768]{1,0:T(8,128)(2,1)} %get-tuple-element.147), channel_id=1, source_target_pairs={{0,31},{1,30},{2,29},{3,28},{4,27},{5,26},{6,25},{7,24},{8,23},{9,... | collective-permute-start | bytes 1179656 | tf_op jit(solution)/shard_map/ppermute | solution.py:729
  16.5 3.7 %all-to-all-start.4 = ((bf16[16,256,128]{2,1,0:T(8,128)(2,1)}), bf16[16,256,128]{2,1,0:T(8,128)(2,1)S(1)}, u32[]{:S(2)}, u32[]{:S(2)}) async-start(bf16[16,256,128]{2,1,0:T(8,128)(2,1)} %get-tuple-element.146), calls=%async_computation.4 | async-start | bytes 2097152 | tf_op jit(solution)/shard_map/all_to_all | solution.py:738
  20.3 10.9 %collective-permute-done.12.received_ref = bf16[256,768]{1,0:T(8,128)(2,1)S(1)} collective-permute-done((bf16[256,768]{1,0:T(8,128)(2,1)}, bf16[256,768]{1,0:T(8,128)(2,1)S(1)}, u32[]{:S(2)}, u32[]{:S(2)}) %collective-permute-start.12) | collective-permute-done | bytes 393248 | tf_op jit(solution)/shard_map/ppermute | solution.py:729
  31.2 2.8 %query_rows.1 = (bf16[256,768]{1,0:T(8,128)(2,1)S(1)}, bf16[256,768]{1,0:T(8,128)(2,1)}, bf16[256,768]{1,0:T(8,128)(2,1)}) custom-call(bf16[256,768]{1,0:T(8,128)(2,1)S(1)} %bitcast.39, bf16[256,768]{1,0:T(8,128)(2,1)S(1)} %collective-permute-done.12.received_ref, f32[768]{0:T(1024)S(1)} %copy-done.20, f32[768]{0:T(1024)S(1)} %copy-done.3, ...), custom_call_target="tpu_custom_call" | custom-call | flops 30000001024 | bytes 1048576 | tf_op jit(solution)/shard_map/query_rows/pallas_call | solution.py:577
  34.1 5.0 %all-to-all-done.4.own_ref = bf16[16,256,128]{2,1,0:T(8,128)(2,1)S(1)} async-done(((bf16[16,256,128]{2,1,0:T(8,128)(2,1)}), bf16[16,256,128]{2,1,0:T(8,128)(2,1)S(1)}, u32[]{:S(2)}, u32[]{:S(2)}) %all-to-all-start.4) | async-done | bytes 1048608 | tf_op jit(solution)/shard_map/all_to_all | solution.py:738
  39.1 0.5 collective-permute-start.16
  39.6 0.2 reduce-window.8
  39.8 0.1 pad_add_fusion
  39.9 0.1 select_reduce_fusion
  40.1 0.2 collective-permute-start.18
  40.3 2.2 collective-permute-done.15.peer_ref
  42.5 18.6 %attend.1 = (bf16[256,768]{1,0:T(8,128)(2,1)S(1)}, f32[2,64,1536]{2,1,0:T(8,128)}, f32[2,1,1536]{2,1,0:T(1,128)S(1)}) custom-call(s32[1]{0:T(128)} %bitcast.16.place_ref, bf16[256,768]{1,0:T(8,128)(2,1)} %get-tuple-element.149.query_ref, bf16[16,256,128]{2,1,0:T(8,128)(2,1)S(1)} %all-to-all-done.4.own_ref, ...), custom_call_target="tpu_custom_call" | custom-call | flops 24999999488 | bytes 8388608 | tf_op jit(solution)/shard_map/attend/pallas_call | solution.py:280
  61.2 1.5 residual.1
  62.7 0.4 collective-permute-start.17
  63.1 1.4 collective-permute-done.17.peer_ref
  64.5 8.3 %mlp.1 = (bf16[1536,768]{1,0:T(8,128)(2,1)}, bf16[768,1536]{1,0:T(8,128)(2,1)}, f32[1,1536]{1,0:T(1,128)}, f32[256,768]{1,0:T(8,128)}, bf16[256,768]{1,0:T(8,128...) custom-call(bf16[256,768]{1,0:T(8,128)(2,1)S(1)} %get-tuple-element.153.own_ref, ...), custom_call_target="tpu_custom_call" | custom-call | flops 10000000000 | bytes 1048576 | tf_op jit(solution)/shard_map/mlp/pallas_call | solution.py:577
  72.9 0.4 collective-permute-start.19
  73.4 1.3 collective-permute-done.19.peer_back_ref
  74.7 2.8 %residual_back.1 = (f32[256,768]{1,0:T(8,128)}, bf16[256,768]{1,0:T(8,128)(2,1)S(1)}, bf16[256,768]{1,0:T(8,128)(2,1)S(1)}, f32[8,768]{1,0:T(8,128)}) custom-call(f32[256,768]{1,0:T(8,128)S(1)} %get-tuple-element.157.back_ref, bf16[256,768]{1,0:T(8,128)(2,1)S(1)} %collective-permute-done.19.peer_back_ref, ...), custom_call_target="tpu_custom_call" | custom-call | flops 1000000000 | bytes 1048576 | tf_op jit(solution)/shard_map/residual_back/pallas_call | solution.py:577
  77.5 138.0 %conditional.1 = (bf16[1,256,768]{2,1,0:T(8,128)(2,1)}, f32[1,256,768]{2,1,0:T(8,128)}, f32[768]{0:T(1024)}, f32[768]{0:T(1024)}, f32[768,384]{1,0:T(8,128)}, /*...) conditional(s32[]{:T(128)} %bitcast.15, () %tuple.18, ...), branch_computations={%region_2.3_spmd, %region_3.6_spmd} | conditional | flops 56006414336 | bytes 75827368 | solution.py:884
  77.6 37.5 %attend_back.1 = (bf16[256,768]{1,0:T(8,128)(2,1)S(1)}, bf16[16,256,128]{2,1,0:T(8,128)(2,1)S(1)}, bf16[16,256,128]{2,1,0:T(8,128)(2,1)S(1)}) custom-call(s32[1]{0:T(128)} %get-tuple-element.50.place_ref, bf16[256,768]{1,0:T(8,128)(2,1)S(1)} %get-tuple-element.51.query_ref, bf16[16,256,128]{2,1,0:T(8,128)(2,1)S(1)} %get-tuple-element.52.own_ref, ...), custom_call_target="tpu_custom_call" | custom-call | flops 44999999488 | bytes 12582912 | tf_op jit(solution)/shard_map/cond/branch_1_fun/attend_back/pallas_call | solution.py:307
  115.1 0.6 collective-permute-start.2
  115.7 3.1 %query_back.1 = (f32[256,768]{1,0:T(8,128)S(1)}, f32[4608,128]{1,0:T(8,128)S(1)}, bf16[4608,128]{1,0:T(8,128)(2,1)}, f32[1,768]{1,0:T(1,128)S(1)}) custom-call(bf16[256,768]{1,0:T(8,128)(2,1)S(1)} %get-tuple-element.60.grad_ref, bf16[256,768]{1,0:T(8,128)(2,1)S(1)} %get-tuple-element.61.normed_ref, bf16[256,768]{1,0:T(8,128)(2,1)S(1)} %get-tuple-element.62.attended_ref, ...), custom_call_target="tpu_custom_call" | custom-call | flops 10000000000 | bytes 1048576 | tf_op jit(solution)/shard_map/cond/branch_1_fun/query_back/pallas_call | solution.py:577
  118.8 0.9 copy-done.12
  119.7 1.2 add_convert_fusion
  120.9 6.0 %all-to-all-start = ((bf16[16,256,128]{2,1,0:T(8,128)(2,1)}), bf16[16,256,128]{2,1,0:T(8,128)(2,1)}, u32[]{:S(2)}, u32[]{:S(2)}) async-start(bf16[16,256,128]{2,1,0:T(8,128)(2,1)} %add_convert_fusion), calls=%async_computation | async-start | bytes 2097152 | tf_op jit(solution)/shard_map/cond/branch_1_fun/all_to_all | solution.py:738
  127.0 1.0 pack.1
  128.1 0.8 copy-done
  128.9 3.2 %collective-permute-start.5 = (bf16[1152,128]{1,0:T(8,128)(2,1)}, bf16[1152,128]{1,0:T(8,128)(2,1)S(1)}, u32[]{:S(2)}, u32[]{:S(2)}) collective-permute-start(bf16[1152,128]{1,0:T(8,128)(2,1)} %get-tuple-element.80), channel_id=1, source_target_pairs={{0,64},{32,96},{64,0},{96,32},{1,65},{33,97},{65,1},{97,33},{2,66}... | collective-permute-start | bytes 884744 | tf_op jit(solution)/shard_map/cond/branch_1_fun/ppermute | solution.py:820
  132.1 0.7 collective-permute-start.6
  132.7 2.6 %collective-permute-start.7 = (bf16[1152,128]{1,0:T(8,128)(2,1)}, bf16[1152,128]{1,0:T(8,128)(2,1)S(1)}, u32[]{:S(2)}, u32[]{:S(2)}) collective-permute-start(bf16[1152,128]{1,0:T(8,128)(2,1)} %get-tuple-element.82), channel_id=1, source_target_pairs={{0,96},{32,0},{64,32},{96,64},{1,97},{33,1},{65,33},{97,65},{2,98}... | collective-permute-start | bytes 884744 | tf_op jit(solution)/shard_map/cond/branch_1_fun/ppermute | solution.py:820
  135.3 10.0 %all-to-all-done.arrived_ref = bf16[16,256,128]{2,1,0:T(8,128)(2,1)} async-done(((bf16[16,256,128]{2,1,0:T(8,128)(2,1)}), bf16[16,256,128]{2,1,0:T(8,128)(2,1)}, u32[]{:S(2)}, u32[]{:S(2)}) %all-to-all-start) | async-done | bytes 1048608 | tf_op jit(solution)/shard_map/cond/branch_1_fun/all_to_all | solution.py:738
  145.3 1.1 copy-done.13
  146.4 3.2 %token_back.1 = (f32[128,768]{1,0:T(8,128)S(1)}, bf16[128,768]{1,0:T(8,128)(2,1)S(1)}, bf16[1024,128]{1,0:T(8,128)(2,1)}) custom-call(bf16[16,256,128]{2,1,0:T(8,128)(2,1)} %all-to-all-done.arrived_ref, f32[256,768]{1,0:T(8,128)S(1)} %copy-done.13, bf16[768,128]{1,0:T(8,128)(2,1)} %get-tuple-element.67.weight_ref, bf16[256,768]{1,0:T(8,128)(2,1)} %copy-done.25, ...), custom_call_target="tpu_custom_call" | custom-call | flops 1000000000 | bytes 1048576 | tf_op jit(solution)/shard_map/cond/branch_1_fun/token_back/pallas_call | solution.py:577
  149.7 4.7 %all-to-all-start.1 = ((bf16[4,256,128]{2,1,0:T(8,128)(2,1)}), bf16[4,256,128]{2,1,0:T(8,128)(2,1)S(1)}, u32[]{:S(2)}, u32[]{:S(2)}) async-start(bf16[4,256,128]{2,1,0:T(8,128)(2,1)} %bitcast.4), calls=%async_computation.1 | async-start | bytes 524288 | tf_op jit(solution)/shard_map/cond/branch_1_fun/all_to_all | solution.py:738
  154.4 0.1 add_convert_fusion.2
  154.6 6.6 %all-to-all-done.1 = bf16[4,256,128]{2,1,0:T(8,128)(2,1)S(1)} async-done(((bf16[4,256,128]{2,1,0:T(8,128)(2,1)}), bf16[4,256,128]{2,1,0:T(8,128)(2,1)S(1)}, u32[]{:S(2)}, u32[]{:S(2)}) %all-to-all-start.1) | async-done | bytes 262176 | tf_op jit(solution)/shard_map/cond/branch_1_fun/all_to_all | solution.py:738
  161.2 0.8 pad_maximum_fusion
  162.0 3.5 %all-to-all-start.2 = ((bf16[16,88,128]{2,1,0:T(8,128)(2,1)}), bf16[16,88,128]{2,1,0:T(8,128)(2,1)S(1)}, u32[]{:S(2)}, u32[]{:S(2)}) async-start(bf16[16,88,128]{2,1,0:T(8,128)(2,1)} %pad_maximum_fusion), calls=%async_computation.2 | async-start | bytes 720896 | tf_op jit(solution)/shard_map/cond/branch_1_fun/all_to_all | solution.py:738
  165.6 0.1 collective-permute-start
  165.7 9.1 %all-to-all-done.2 = bf16[16,88,128]{2,1,0:T(8,128)(2,1)S(1)} async-done(((bf16[16,88,128]{2,1,0:T(8,128)(2,1)}), bf16[16,88,128]{2,1,0:T(8,128)(2,1)S(1)}, u32[]{:S(2)}, u32[]{:S(2)}) %all-to-all-start.2) | async-done | bytes 360480 | tf_op jit(solution)/shard_map/cond/branch_1_fun/all_to_all | solution.py:738
  174.8 0.1 collective-permute-start.8
  174.9 1.1 collective-permute-done.8
  176.1 0.8 broadcast_in_dim.22
  176.9 3.5 %all-to-all-start.3 = ((bf16[16,88,128]{2,1,0:T(8,128)(2,1)}), bf16[16,88,128]{2,1,0:T(8,128)(2,1)S(1)}, u32[]{:S(2)}, u32[]{:S(2)}) async-start(bf16[16,88,128]{2,1,0:T(8,128)(2,1)} %broadcast_in_dim.22), calls=%async_computation.3 | async-start | bytes 720896 | tf_op jit(solution)/shard_map/cond/branch_1_fun/all_to_all | solution.py:738
  180.5 0.1 add_convert_fusion.1
  180.7 4.8 %collective-permute-start.1 = (bf16[128,768]{1,0:T(8,128)(2,1)S(1)}, bf16[128,768]{1,0:T(8,128)(2,1)S(1)}, u32[]{:S(2)}, u32[]{:S(2)}) collective-permute-start(bf16[128,768]{1,0:T(8,128)(2,1)S(1)} %get-tuple-element.190), channel_id=1, source_target_pairs={{0,31},{1,30},{2,29},{3,28},{4,27},{5,26},{6,25},{7,24},{8,23},{9,... | collective-permute-start | bytes 589832 | tf_op jit(solution)/shard_map/cond/branch_1_fun/ppermute | solution.py:729
  185.5 6.8 %all-to-all-done.3.own_ref = bf16[16,88,128]{2,1,0:T(8,128)(2,1)S(1)} async-done(((bf16[16,88,128]{2,1,0:T(8,128)(2,1)}), bf16[16,88,128]{2,1,0:T(8,128)(2,1)S(1)}, u32[]{:S(2)}, u32[]{:S(2)}) %all-to-all-start.3) | async-done | bytes 360480 | tf_op jit(solution)/shard_map/cond/branch_1_fun/all_to_all | solution.py:738
  192.3 1.3 collective-permute-start.11
  193.6 1.5 collective-permute-start.10
  195.1 1.7 collective-permute-done.1
  196.7 0.8 maximum_bitcast_fusion.1
  197.5 6.7 %collective-permute-done.3 = bf16[128,768]{1,0:T(8,128)(2,1)S(1)} collective-permute-done((bf16[128,768]{1,0:T(8,128)(2,1)S(1)}, bf16[128,768]{1,0:T(8,128)(2,1)S(1)}, u32[]{:S(2)}, u32[]{:S(2)}) %collective-permute-start.3) | collective-permute-done | bytes 196640 | tf_op jit(solution)/shard_map/cond/branch_1_fun/ppermute | solution.py:729
  204.2 0.9 maximum_bitcast_fusion
  205.1 1.3 collective-permute-done.10.second_ref
  206.4 5.5 %collective-permute-done.9.first_ref = bf16[16,88,128]{2,1,0:T(8,128)(2,1)S(1)} collective-permute-done((bf16[16,88,128]{2,1,0:T(8,128)(2,1)S(1)}, bf16[16,88,128]{2,1,0:T(8,128)(2,1)S(1)}, u32[]{:S(2)}, u32[]{:S(2)}) %collective-permute-start.9) | collective-permute-done | bytes 360480 | tf_op jit(solution)/shard_map/cond/branch_1_fun/ppermute | solution.py:845
  212.0 1.8 unpack.1
  213.8 0.6 slice_bitcast_fusion.7
  214.4 0.6 select_bitcast_fusion
  215.0 0.6 slice_bitcast_fusion.1
  215.6 14.1 %all-reduce.3.cloned.1.call-done = (bf16[1536,768]{1,0:T(8,128)(2,1)}, bf16[768,1536]{1,0:T(8,128)(2,1)}) async-done(((bf16[1536,768]{1,0:T(8,128)(2,1)}, bf16[768,1536]{1,0:T(8,128)(2,1)}), (bf16[1536,768]{1,0:T(8,128)(2,1)}, bf16[768,1536]{1,0:T(8,128)(2,1)})) %all-reduce.3.cloned.1.call-update) | async-done | bytes 4718608 | tf_op jit(solution)/shard_map/psum | solution.py:797
  229.7 5.5 %widen.1 = (f32[1536,768]{1,0:T(8,128)}, f32[768,1536]{1,0:T(8,128)}) custom-call(bf16[1536,768]{1,0:T(8,128)(2,1)} %get-tuple-element.187.contract_ref, bf16[768,1536]{1,0:T(8,128)(2,1)} %get-tuple-element.188.expand_ref), custom_call_target="tpu_custom_call" | custom-call | tf_op jit(solution)/shard_map/widen/pallas_call | solution.py:641
  (97 shorter events, 0.7 us)
Async XLA Ops:
  7.2 24.0 %copy-start.20 = (f32[768]{0:T(1024)S(1)}, f32[768]{0:T(1024)}, u32[]{:S(2)}) copy-start(f32[768]{0:T(1024)} %gain_ref.5) | copy-start | bytes 9220
  7.2 24.0 %copy-start.3 = (f32[768]{0:T(1024)S(1)}, f32[768]{0:T(1024)}, u32[]{:S(2)}) copy-start(f32[768]{0:T(1024)} %shift_ref.4) | copy-start | bytes 9220
  7.2 24.0 %copy-start.2 = (bf16[1,256,768]{2,1,0:T(8,128)(2,1)S(1)}, bf16[1,256,768]{2,1,0:T(8,128)(2,1)}, u32[]{:S(2)}) copy-start(bf16[1,256,768]{2,1,0:T(8,128)(2,1)} %param.19) | copy-start | bytes 1179652
  7.2 24.0 %copy-start.11 = (f32[384]{0:T(512)S(1)}, f32[384]{0:T(512)}, u32[]{:S(2)}) copy-start(f32[384]{0:T(512)} %mine_bias_ref.1) | copy-start | bytes 4612
  7.2 24.0 %collective-permute-start.13 = (bf16[768,384]{1,0:T(8,128)(2,1)}, bf16[768,384]{1,0:T(8,128)(2,1)}, u32[]{:S(2)}, u32[]{:S(2)}) collective-permute-start(bf16[768,384]{1,0:T(8,128)(2,1)} %mine_ref.3), channel_id=1, source_target_pairs={{0,1},{1,0},{2,3},{3,2},{4,5},{5,4},{6,7},{7,6},{8,9},{9,8},{10,11... | collective-permute-start | bytes 1769480 | tf_op jit(solution)/shard_map/ppermute | solution.py:724
  10.1 21.1 %collective-permute-start.12 = (bf16[256,768]{1,0:T(8,128)(2,1)}, bf16[256,768]{1,0:T(8,128)(2,1)S(1)}, u32[]{:S(2)}, u32[]{:S(2)}) collective-permute-start(bf16[256,768]{1,0:T(8,128)(2,1)} %get-tuple-element.147), channel_id=1, source_target_pairs={{0,31},{1,30},{2,29},{3,28},{4,27},{5,26},{6,25},{7,24},{8,23},{9,... | collective-permute-start | bytes 1179656 | tf_op jit(solution)/shard_map/ppermute | solution.py:729
  16.5 3.8 %collective-permute-start.14 = (f32[384]{0:T(512)}, f32[384]{0:T(512)S(1)}, u32[]{:S(2)}, u32[]{:S(2)}) collective-permute-start(f32[384]{0:T(512)} %mine_bias_ref.1), channel_id=1, source_target_pairs={{0,1},{1,0},{2,3},{3,2},{4,5},{5,4},{6,7},{7,6},{8,9},{9,8},{10,11... | collective-permute-start | bytes 4616 | tf_op jit(solution)/shard_map/ppermute | solution.py:724
  16.5 22.5 %all-to-all-start.4 = ((bf16[16,256,128]{2,1,0:T(8,128)(2,1)}), bf16[16,256,128]{2,1,0:T(8,128)(2,1)S(1)}, u32[]{:S(2)}, u32[]{:S(2)}) async-start(bf16[16,256,128]{2,1,0:T(8,128)(2,1)} %get-tuple-element.146), calls=%async_computation.4 | async-start | bytes 2097152 | tf_op jit(solution)/shard_map/all_to_all | solution.py:738
  20.2 18.9 %copy-start.6 = (bf16[384,768]{1,0:T(8,128)(2,1)S(1)}, bf16[384,768]{1,0:T(8,128)(2,1)}, u32[]{:S(2)}) copy-start(bf16[384,768]{1,0:T(8,128)(2,1)} %mine_ref.5) | copy-start | bytes 1769476
  20.2 19.4 %copy-start.24 = (s32[1,8]{1,0:T(1,128)S(1)}, s32[1,8]{1,0:T(1,128)}, u32[]{:S(2)}) copy-start(s32[1,8]{1,0:T(1,128)} %param.35) | copy-start | bytes 100
  20.2 19.8 %copy-start.16 = (bf16[1,256,768]{2,1,0:T(8,128)(2,1)S(1)}, bf16[1,256,768]{2,1,0:T(8,128)(2,1)}, u32[]{:S(2)}) copy-start(bf16[1,256,768]{2,1,0:T(8,128)(2,1)} %param.34) | copy-start | bytes 1179652
  20.2 209.4 %all-reduce.3.cloned.1.call-start = ((), (), s32[]{:S(2)}) async-start(), calls=%async_computation.5 | async-start | bytes 9437184 | tf_op jit(solution)/shard_map/psum | solution.py:797
  39.1 22.1 %copy-start.14 = (bf16[16,256,128]{2,1,0:T(8,128)(2,1)}, bf16[16,256,128]{2,1,0:T(8,128)(2,1)S(1)}, u32[]{:S(2)}) copy-start(bf16[16,256,128]{2,1,0:T(8,128)(2,1)S(1)} %all-to-all-done.4.own_ref) | copy-start | bytes 3145732
  39.1 3.4 %collective-permute-start.15 = (bf16[16,256,128]{2,1,0:T(8,128)(2,1)S(1)}, bf16[16,256,128]{2,1,0:T(8,128)(2,1)}, u32[]{:S(2)}, u32[]{:S(2)}) collective-permute-start(bf16[16,256,128]{2,1,0:T(8,128)(2,1)S(1)} %all-to-all-done.4.own_ref), channel_id=1, source_target_pairs={{0,1},{1,0},{2,3},{3,2},{4,5},{5,4},{6,7},{7,6},{8,9},{9,8},{10,11... | collective-permute-start | bytes 3145736 | tf_op jit(solution)/shard_map/ppermute | solution.py:724
  39.1 22.1 %collective-permute-start.16 = (bf16[384,768]{1,0:T(8,128)(2,1)S(1)}, bf16[384,768]{1,0:T(8,128)(2,1)S(1)}, u32[]{:S(2)}, u32[]{:S(2)}) collective-permute-start(bf16[384,768]{1,0:T(8,128)(2,1)S(1)} %copy-done.6), channel_id=1, source_target_pairs={{0,1},{1,0},{2,3},{3,2},{4,5},{5,4},{6,7},{7,6},{8,9},{9,8},{10,11... | collective-permute-start | bytes 1769480 | tf_op jit(solution)/shard_map/ppermute | solution.py:724
  40.1 23.0 %collective-permute-start.18 = (bf16[256,768]{1,0:T(8,128)(2,1)S(1)}, bf16[256,768]{1,0:T(8,128)(2,1)S(1)}, u32[]{:S(2)}, u32[]{:S(2)}) collective-permute-start(bf16[256,768]{1,0:T(8,128)(2,1)S(1)} %pad_maximum_fusion.2.own_grad_ref.grad_ref), channel_id=1, source_target_pairs={{0,1},{1,0},{2,3},{3,2},{4,5},{5,4},{6,7},{7,6},{8,9},{9,8},{10,11... | collective-permute-start | bytes 1179656 | tf_op jit(solution)/shard_map/ppermute | solution.py:724
  42.5 18.7 %copy-start.8 = (f32[768]{0:T(1024)S(1)}, f32[768]{0:T(1024)}, u32[]{:S(2)}) copy-start(f32[768]{0:T(1024)} %bias_ref.4) | copy-start | bytes 9220
  42.5 18.7 %copy-start.9 = (f32[768]{0:T(1024)S(1)}, f32[768]{0:T(1024)}, u32[]{:S(2)}) copy-start(f32[768]{0:T(1024)} %shift_ref.5) | copy-start | bytes 9220
  42.5 18.7 %copy-start.10 = (f32[768]{0:T(1024)S(1)}, f32[768]{0:T(1024)}, u32[]{:S(2)}) copy-start(f32[768]{0:T(1024)} %gain_ref.7) | copy-start | bytes 9220
  42.5 22.0 %copy-start.5 = (bf16[1536,768]{1,0:T(8,128)(2,1)S(1)}, bf16[1536,768]{1,0:T(8,128)(2,1)}, u32[]{:S(2)}) copy-start(bf16[1536,768]{1,0:T(8,128)(2,1)} %contract_ref.1) | copy-start | bytes 7077892
  61.1 2.0 copy-start.29
  61.2 3.3 %copy-start.4 = (bf16[768,1536]{1,0:T(8,128)(2,1)S(1)}, bf16[768,1536]{1,0:T(8,128)(2,1)}, u32[]{:S(2)}) copy-start(bf16[768,1536]{1,0:T(8,128)(2,1)} %expand_ref.1) | copy-start | bytes 7077892
  61.2 3.3 %copy-start.7 = (f32[1536]{0:T(1024)S(1)}, f32[1536]{0:T(1024)}, u32[]{:S(2)}) copy-start(f32[1536]{0:T(1024)} %bias_ref.5) | copy-start | bytes 18436
  62.7 1.7 collective-permute-start.17
  72.8 4.7 %copy-start.15 = (bf16[16,256,128]{2,1,0:T(8,128)(2,1)S(1)}, bf16[16,256,128]{2,1,0:T(8,128)(2,1)}, u32[]{:S(2)}) copy-start(bf16[16,256,128]{2,1,0:T(8,128)(2,1)} %copy-done.14) | copy-start | bytes 3145732
  72.8 4.7 %copy-start.22 = (bf16[768,384]{1,0:T(8,128)(2,1)S(1)}, bf16[768,384]{1,0:T(8,128)(2,1)}, u32[]{:S(2)}) copy-start(bf16[768,384]{1,0:T(8,128)(2,1)} %mine_ref.3) | copy-start | bytes 1769476
  72.8 4.7 %copy-start.26 = (bf16[256,768]{1,0:T(8,128)(2,1)S(1)}, bf16[256,768]{1,0:T(8,128)(2,1)}, u32[]{:S(2)}) copy-start(bf16[256,768]{1,0:T(8,128)(2,1)} %get-tuple-element.162) | copy-start | bytes 1179652
  72.9 4.7 %copy-start.30 = (bf16[256,768]{1,0:T(8,128)(2,1)S(1)}, bf16[256,768]{1,0:T(8,128)(2,1)}, u32[]{:S(2)}) copy-start(bf16[256,768]{1,0:T(8,128)(2,1)} %copy-done.29) | copy-start | bytes 1179652
  72.9 4.7 %copy-start.31 = (f32[2,64,1536]{2,1,0:T(8,128)S(1)}, f32[2,64,1536]{2,1,0:T(8,128)}, u32[]{:S(2)}) copy-start(f32[2,64,1536]{2,1,0:T(8,128)} %get-tuple-element.160) | copy-start | bytes 2359300
  72.9 4.7 %copy-start.32 = (bf16[256,768]{1,0:T(8,128)(2,1)S(1)}, bf16[256,768]{1,0:T(8,128)(2,1)}, u32[]{:S(2)}) copy-start(bf16[256,768]{1,0:T(8,128)(2,1)} %get-tuple-element.149.query_ref) | copy-start | bytes 1179652
  72.9 1.8 collective-permute-start.19
  77.6 37.5 %copy-start.25 = (bf16[256,768]{1,0:T(8,128)(2,1)}, bf16[256,768]{1,0:T(8,128)(2,1)S(1)}, u32[]{:S(2)}) copy-start(bf16[256,768]{1,0:T(8,128)(2,1)S(1)} %get-tuple-element.68.tokens_ref) | copy-start | bytes 1179652 | tf_op jit(solution)/shard_map/cond
  77.6 38.1 %copy-start.27 = (bf16[256,768]{1,0:T(8,128)(2,1)}, bf16[256,768]{1,0:T(8,128)(2,1)S(1)}, u32[]{:S(2)}) copy-start(bf16[256,768]{1,0:T(8,128)(2,1)S(1)} %get-tuple-element.61.normed_ref) | copy-start | bytes 1179652 | tf_op jit(solution)/shard_map/cond
  115.1 4.6 %collective-permute-start.2 = (bf16[16,256,128]{2,1,0:T(8,128)(2,1)S(1)}, bf16[16,256,128]{2,1,0:T(8,128)(2,1)S(1)}, u32[]{:S(2)}, u32[]{:S(2)}) collective-permute-start(bf16[16,256,128]{2,1,0:T(8,128)(2,1)S(1)} %get-tuple-element.59), channel_id=1, source_target_pairs={{0,1},{1,0},{2,3},{3,2},{4,5},{5,4},{6,7},{7,6},{8,9},{9,8},{10,11... | collective-permute-start | bytes 3145736 | tf_op jit(solution)/shard_map/cond/branch_1_fun/ppermute | solution.py:724
  118.8 0.9 copy-start.12
  119.6 7.4 %collective-permute-start.4 = (bf16[4608,128]{1,0:T(8,128)(2,1)}, bf16[4608,128]{1,0:T(8,128)(2,1)S(1)}, u32[]{:S(2)}, u32[]{:S(2)}) collective-permute-start(bf16[4608,128]{1,0:T(8,128)(2,1)} %get-tuple-element.77), channel_id=1, source_target_pairs={{0,1},{1,0},{2,3},{3,2},{4,5},{5,4},{6,7},{7,6},{8,9},{9,8},{10,11... | collective-permute-start | bytes 3538952 | tf_op jit(solution)/shard_map/cond/branch_1_fun/ppermute | solution.py:724
  120.9 24.4 %all-to-all-start = ((bf16[16,256,128]{2,1,0:T(8,128)(2,1)}), bf16[16,256,128]{2,1,0:T(8,128)(2,1)}, u32[]{:S(2)}, u32[]{:S(2)}) async-start(bf16[16,256,128]{2,1,0:T(8,128)(2,1)} %add_convert_fusion), calls=%async_computation | async-start | bytes 2097152 | tf_op jit(solution)/shard_map/cond/branch_1_fun/all_to_all | solution.py:738
  127.0 18.3 %copy-start.28 = (f32[1,1536]{1,0:T(1,128)S(1)}, f32[1,1536]{1,0:T(1,128)}, u32[]{:S(2)}) copy-start(f32[1,1536]{1,0:T(1,128)} %get-tuple-element.73.expand_bias_ref) | copy-start | bytes 18436 | tf_op jit(solution)/shard_map/cond
  128.1 0.8 copy-start
  128.9 20.8 %collective-permute-start.5 = (bf16[1152,128]{1,0:T(8,128)(2,1)}, bf16[1152,128]{1,0:T(8,128)(2,1)S(1)}, u32[]{:S(2)}, u32[]{:S(2)}) collective-permute-start(bf16[1152,128]{1,0:T(8,128)(2,1)} %get-tuple-element.80), channel_id=1, source_target_pairs={{0,64},{32,96},{64,0},{96,32},{1,65},{33,97},{65,1},{97,33},{2,66}... | collective-permute-start | bytes 884744 | tf_op jit(solution)/shard_map/cond/branch_1_fun/ppermute | solution.py:820
  132.1 17.6 %collective-permute-start.6 = (bf16[1152,128]{1,0:T(8,128)(2,1)}, bf16[1152,128]{1,0:T(8,128)(2,1)S(1)}, u32[]{:S(2)}, u32[]{:S(2)}) collective-permute-start(bf16[1152,128]{1,0:T(8,128)(2,1)} %get-tuple-element.81), channel_id=1, source_target_pairs={{0,32},{32,64},{64,96},{96,0},{1,33},{33,65},{65,97},{97,1},{2,34}... | collective-permute-start | bytes 884744 | tf_op jit(solution)/shard_map/cond/branch_1_fun/ppermute | solution.py:820
  132.7 16.9 %collective-permute-start.7 = (bf16[1152,128]{1,0:T(8,128)(2,1)}, bf16[1152,128]{1,0:T(8,128)(2,1)S(1)}, u32[]{:S(2)}, u32[]{:S(2)}) collective-permute-start(bf16[1152,128]{1,0:T(8,128)(2,1)} %get-tuple-element.82), channel_id=1, source_target_pairs={{0,96},{32,0},{64,32},{96,64},{1,97},{33,1},{65,33},{97,65},{2,98}... | collective-permute-start | bytes 884744 | tf_op jit(solution)/shard_map/cond/branch_1_fun/ppermute | solution.py:820
  145.3 1.1 copy-start.13
  146.4 8.0 %copy-start.1 = (f32[1152,128]{1,0:T(8,128)S(1)}, f32[1152,128]{1,0:T(8,128)}, u32[]{:S(2)}) copy-start(f32[1152,128]{1,0:T(8,128)} %copy-done) | copy-start | bytes 1769476 | tf_op jit(solution)/shard_map/cond
  149.7 15.9 %copy-start.23 = (bf16[256,768]{1,0:T(8,128)(2,1)S(1)}, bf16[256,768]{1,0:T(8,128)(2,1)}, u32[]{:S(2)}) copy-start(bf16[256,768]{1,0:T(8,128)(2,1)} %get-tuple-element.48) | copy-start | bytes 1179652 | tf_op jit(solution)/shard_map/cond
  149.7 11.5 %all-to-all-start.1 = ((bf16[4,256,128]{2,1,0:T(8,128)(2,1)}), bf16[4,256,128]{2,1,0:T(8,128)(2,1)S(1)}, u32[]{:S(2)}, u32[]{:S(2)}) async-start(bf16[4,256,128]{2,1,0:T(8,128)(2,1)} %bitcast.4), calls=%async_computation.1 | async-start | bytes 524288 | tf_op jit(solution)/shard_map/cond/branch_1_fun/all_to_all | solution.py:738
  154.5 26.0 %copy-start.17 = (f32[256,768]{1,0:T(8,128)S(1)}, f32[256,768]{1,0:T(8,128)}, u32[]{:S(2)}) copy-start(f32[256,768]{1,0:T(8,128)} %get-tuple-element.46) | copy-start | bytes 2359300 | tf_op jit(solution)/shard_map/cond
  154.5 26.0 %copy-start.18 = (f32[256,768]{1,0:T(8,128)S(1)}, f32[256,768]{1,0:T(8,128)}, u32[]{:S(2)}) copy-start(f32[256,768]{1,0:T(8,128)} %get-tuple-element.47) | copy-start | bytes 2359300 | tf_op jit(solution)/shard_map/cond
  154.5 26.0 %copy-start.21 = (f32[768]{0:T(1024)S(1)}, f32[768]{0:T(1024)}, u32[]{:S(2)}) copy-start(f32[768]{0:T(1024)} %get-tuple-element.186) | copy-start | bytes 9220 | tf_op jit(solution)/shard_map/cond
  162.0 12.7 %all-to-all-start.2 = ((bf16[16,88,128]{2,1,0:T(8,128)(2,1)}), bf16[16,88,128]{2,1,0:T(8,128)(2,1)S(1)}, u32[]{:S(2)}, u32[]{:S(2)}) async-start(bf16[16,88,128]{2,1,0:T(8,128)(2,1)} %pad_maximum_fusion), calls=%async_computation.2 | async-start | bytes 720896 | tf_op jit(solution)/shard_map/cond/branch_1_fun/all_to_all | solution.py:738
  165.6 14.9 %collective-permute-start = (bf16[256,768]{1,0:T(8,128)(2,1)S(1)}, bf16[256,768]{1,0:T(8,128)(2,1)S(1)}, u32[]{:S(2)}, u32[]{:S(2)}) collective-permute-start(bf16[256,768]{1,0:T(8,128)(2,1)S(1)} %copy-done.23), channel_id=1, source_target_pairs={{0,1},{1,0},{2,3},{3,2},{4,5},{5,4},{6,7},{7,6},{8,9},{9,8},{10,11... | collective-permute-start | bytes 1179656 | tf_op jit(solution)/shard_map/cond/branch_1_fun/ppermute | solution.py:724
  174.8 1.3 collective-permute-start.8
  176.9 15.3 %all-to-all-start.3 = ((bf16[16,88,128]{2,1,0:T(8,128)(2,1)}), bf16[16,88,128]{2,1,0:T(8,128)(2,1)S(1)}, u32[]{:S(2)}, u32[]{:S(2)}) async-start(bf16[16,88,128]{2,1,0:T(8,128)(2,1)} %broadcast_in_dim.22), calls=%async_computation.3 | async-start | bytes 720896 | tf_op jit(solution)/shard_map/cond/branch_1_fun/all_to_all | solution.py:738
  180.7 16.0 %collective-permute-start.1 = (bf16[128,768]{1,0:T(8,128)(2,1)S(1)}, bf16[128,768]{1,0:T(8,128)(2,1)S(1)}, u32[]{:S(2)}, u32[]{:S(2)}) collective-permute-start(bf16[128,768]{1,0:T(8,128)(2,1)S(1)} %get-tuple-element.190), channel_id=1, source_target_pairs={{0,31},{1,30},{2,29},{3,28},{4,27},{5,26},{6,25},{7,24},{8,23},{9,... | collective-permute-start | bytes 589832 | tf_op jit(solution)/shard_map/cond/branch_1_fun/ppermute | solution.py:729
  192.3 12.9 %collective-permute-start.11 = (bf16[16,88,128]{2,1,0:T(8,128)(2,1)S(1)}, bf16[16,88,128]{2,1,0:T(8,128)(2,1)S(1)}, u32[]{:S(2)}, u32[]{:S(2)}) collective-permute-start(bf16[16,88,128]{2,1,0:T(8,128)(2,1)S(1)} %all-to-all-done.3.own_ref), channel_id=1, source_target_pairs={{0,96},{32,0},{64,32},{96,64},{1,97},{33,1},{65,33},{97,65},{2,98}... | collective-permute-start | bytes 1081352 | tf_op jit(solution)/shard_map/cond/branch_1_fun/ppermute | solution.py:845
  193.6 12.9 %collective-permute-start.10 = (bf16[16,88,128]{2,1,0:T(8,128)(2,1)S(1)}, bf16[16,88,128]{2,1,0:T(8,128)(2,1)S(1)}, u32[]{:S(2)}, u32[]{:S(2)}) collective-permute-start(bf16[16,88,128]{2,1,0:T(8,128)(2,1)S(1)} %all-to-all-done.3.own_ref), channel_id=1, source_target_pairs={{0,64},{32,96},{64,0},{96,32},{1,65},{33,97},{65,1},{97,33},{2,66}... | collective-permute-start | bytes 1081352 | tf_op jit(solution)/shard_map/cond/branch_1_fun/ppermute | solution.py:845
  195.1 16.9 %collective-permute-start.9 = (bf16[16,88,128]{2,1,0:T(8,128)(2,1)S(1)}, bf16[16,88,128]{2,1,0:T(8,128)(2,1)S(1)}, u32[]{:S(2)}, u32[]{:S(2)}) collective-permute-start(bf16[16,88,128]{2,1,0:T(8,128)(2,1)S(1)} %all-to-all-done.3.own_ref), channel_id=1, source_target_pairs={{0,32},{32,64},{64,96},{96,0},{1,33},{33,65},{65,97},{97,1},{2,34}... | collective-permute-start | bytes 1081352 | tf_op jit(solution)/shard_map/cond/branch_1_fun/ppermute | solution.py:845
  195.1 9.1 %collective-permute-start.3 = (bf16[128,768]{1,0:T(8,128)(2,1)S(1)}, bf16[128,768]{1,0:T(8,128)(2,1)S(1)}, u32[]{:S(2)}, u32[]{:S(2)}) collective-permute-start(bf16[128,768]{1,0:T(8,128)(2,1)S(1)} %get-tuple-element.75), channel_id=1, source_target_pairs={{0,31},{1,30},{2,29},{3,28},{4,27},{5,26},{6,25},{7,24},{8,23},{9,... | collective-permute-start | bytes 589832 | tf_op jit(solution)/shard_map/cond/branch_1_fun/ppermute | solution.py:729
  215.6 19.6 %copy-start.19 = (f32[1536]{0:T(1024)}, f32[1536]{0:T(1024)S(1)}, u32[]{:S(2)}) copy-start(f32[1536]{0:T(1024)S(1)} %get-tuple-element.143) | copy-start | bytes 18436
Sparse Core Ops, SparseCore 0:
  72.9 156.6 all-reduce.2
